TPU v7x, 128 devices: a whole 4x4x4 slice. The times are simulated.
128 devices in a mesh: section: 2 (over x_lo), shard: 16 (over z, y), replica: 4 (over x_hi, core).
Axes of the slice: x: 4 (x_hi: 2, x_lo: 2; x = x_hi * 2 + x_lo), y: 4, z: 4, core: 2. Of those that a mesh axis runs over, the one named last changes fastest.
Arguments:
- inputs: bfloat16 [2, 4, 2048, 576], P(None, 'replica', 'shard'), may hold values from -6 to 6
- out_grad: bfloat16 [2, 4, 2048, 576], P(None, 'replica', 'shard'), may hold values from -6 to 6
- w_query: bfloat16 [2, 576, 576], P('section', 'shard'), may hold values from -0.25 to 0.25
- w_key: bfloat16 [2, 576, 192], P('section', 'shard'), may hold values from -0.25 to 0.25
- w_value: bfloat16 [2, 576, 192], P('section', 'shard'), may hold values from -0.25 to 0.25
- w_out: bfloat16 [2, 576, 576], P('section', 'shard'), may hold values from -3 to 3
- w_gate: bfloat16 [2, 576, 1536], P('section', 'shard'), may hold values from -0.25 to 0.25
- w_up: bfloat16 [2, 576, 1536], P('section', 'shard'), may hold values from -0.25 to 0.25
- w_down: bfloat16 [2, 1536, 576], P('section', 'shard'), may hold values from -0.15625 to 0.15625
- gain_attn: bfloat16 [2, 576], P('section', 'shard'), may hold values from 0.099609375 to 1.8984375
- gain_ffn: bfloat16 [2, 576], P('section', 'shard'), may hold values from 0.099609375 to 1.8984375
Outputs:
- section_out: bfloat16 [2, 2, 4, 2048, 576], P('section', None, 'replica', 'shard')
- section_in_grad: float32 [2, 2, 4, 2048, 576], P('section', None, 'replica', 'shard')
- grad_query: float32 [2, 576, 576], P('section', 'shard')
- grad_key: float32 [2, 576, 192], P('section', 'shard')
- grad_value: float32 [2, 576, 192], P('section', 'shard')
- grad_out: float32 [2, 576, 576], P('section', 'shard')
- grad_gate: float32 [2, 576, 1536], P('section', 'shard')
- grad_up: float32 [2, 576, 1536], P('section', 'shard')
- grad_down: float32 [2, 1536, 576], P('section', 'shard')
- grad_gain_attn: float32 [2, 576], P('section', 'shard')
- grad_gain_ffn: float32 [2, 576], P('section', 'shard')
All inputs are finite; a program needn't handle non-finite values.
Results may differ from a plain program's by a relative error of at most 0.028.
Values may be sent and summed in bfloat16 or wider, within the bound.
A program may use at most 192 MiB of HBM per device.

v0:
```python
import jax
import jax.numpy as jnp
from jax import lax
from jax.sharding import PartitionSpec as P

HEADS = 9
KV_HEADS = 3
HEAD_DIM = 64


epsilon = 1e-05
rope_base = 100000.0
score_scale = 0.125


def from_behind(block, axis, distance):
    devices = range(lax.axis_size(axis))
    route = [(i - distance, i) for i in devices if i - distance in devices]
    return lax.ppermute(block, axis, route)


def rope_tables(positions, head_size):
    half_size = head_size // 2
    inverse = rope_base ** (-(jnp.arange(half_size, dtype=jnp.float32) * 2.0 / head_size))
    angles = positions.astype(jnp.float32)[:, None] * inverse[None, :]
    angles = jnp.concatenate([angles, angles], axis=1)
    return (jnp.cos(angles), jnp.sin(angles))


def rotate(values, cosine, sine):
    half_size = values.shape[-1] // 2
    turned = jnp.concatenate([-values[..., half_size:], values[..., :half_size]], axis=-1)
    return values * cosine[:, None, :] + turned * sine[:, None, :]


def rotate_back(grads_in, cosine, sine):
    half_size = grads_in.shape[-1] // 2
    scaled = grads_in * sine[:, None, :]
    turned = jnp.concatenate([scaled[..., half_size:], -scaled[..., :half_size]], axis=-1)
    return grads_in * cosine[:, None, :] + turned


def project(left, right):
    return jnp.einsum("scd,de->sce", left, right, preferred_element_type=jnp.float32)


def project_back(left, right):
    return jnp.einsum("sce,de->scd", left, right, preferred_element_type=jnp.float32)


def outer_sum(left, right):
    return jnp.einsum("scd,sce->de", left, right, preferred_element_type=jnp.float32)


def norm_forward(values, gain):
    factor = lax.rsqrt(jnp.mean(values * values, axis=-1, keepdims=True) + epsilon)
    return (values * factor * gain, factor)


def norm_backward(values, factor, gain, upstream):
    scaled = gain * upstream
    grad_gain = jnp.sum(upstream * values * factor, axis=(0, 1))
    grad_values = factor * scaled - values * factor**3 * jnp.mean(
        scaled * values, axis=-1, keepdims=True
    )
    return (grad_values, grad_gain)


def causal_scores(query_blk, key_blk, query_pos):
    scores = (
        jnp.einsum("qhgd,khd->hgqk", query_blk, key_blk, preferred_element_type=jnp.float32)
        * score_scale
    )
    key_pos = jnp.arange(key_blk.shape[0], dtype=jnp.int32)
    causal = key_pos[None, :] <= query_pos[:, None]
    return jnp.where(causal, scores, -1e30)


def attend(query_pos, blocks):
    query_blk, key_blk, value_blk = blocks
    scores = causal_scores(query_blk, key_blk, query_pos)
    peak = jnp.max(scores, axis=-1, keepdims=True)
    powered = jnp.exp(scores - peak)
    weight_sum = jnp.sum(powered, axis=-1, keepdims=True)
    probs = powered / weight_sum
    mixed = jnp.einsum(
        "hgqk,khd->qhgd", probs.astype(jnp.bfloat16), value_blk, preferred_element_type=jnp.float32
    )
    return (mixed, (peak + jnp.log(weight_sum))[..., 0])


def attend_back(query_pos, blocks):
    query_blk, key_blk, value_blk, lse_blk, grad_blk = blocks
    scores = causal_scores(query_blk, key_blk, query_pos)
    probs = jnp.exp(scores - lse_blk[..., None])
    grad_probs = jnp.einsum(
        "qhgd,khd->hgqk", grad_blk, value_blk, preferred_element_type=jnp.float32
    )
    inner_sum = jnp.sum(probs * grad_probs, axis=-1, keepdims=True)
    grad_scores = (probs * (grad_probs - inner_sum)).astype(jnp.bfloat16)
    grad_query = (
        jnp.einsum("hgqk,khd->qhgd", grad_scores, key_blk, preferred_element_type=jnp.float32)
        * score_scale
    )
    grad_key = (
        jnp.einsum("hgqk,qhgd->khd", grad_scores, query_blk, preferred_element_type=jnp.float32)
        * score_scale
    )
    grad_value = jnp.einsum(
        "hgqk,qhgd->khd", probs.astype(jnp.bfloat16), grad_blk, preferred_element_type=jnp.float32
    )
    return (grad_query, grad_key, grad_value)


def layer_forward(hidden_in, weights, cosine, sine, query_pos):
    w_query, w_key, w_value, w_out, w_gate, w_up, w_down, gain_attn, gain_ffn = weights
    seqs_here, span_len, model_width = hidden_in.shape
    group_size = HEADS // KV_HEADS
    normed, factor_attn = norm_forward(hidden_in, gain_attn.astype(jnp.float32))
    normed_b = normed.astype(jnp.bfloat16)
    query_pre = project(normed_b, w_query).reshape(seqs_here, span_len, HEADS, HEAD_DIM)
    queries = (
        rotate(query_pre, cosine, sine)
        .astype(jnp.bfloat16)
        .reshape(seqs_here, span_len, KV_HEADS, group_size, HEAD_DIM)
    )
    key_pre = project(normed_b, w_key).reshape(seqs_here, span_len, KV_HEADS, HEAD_DIM)
    keys_local = (
        rotate(key_pre, cosine, sine)
        .astype(jnp.bfloat16)
        .reshape(seqs_here, span_len, KV_HEADS * HEAD_DIM)
    )
    values_local = project(normed_b, w_value).astype(jnp.bfloat16)
    keys_all, values_all = (
        lax.all_gather(keys_local, "shard", axis=1, tiled=True),
        lax.all_gather(values_local, "shard", axis=1, tiled=True),
    )
    total_len = keys_all.shape[1]
    key_heads = keys_all.reshape(seqs_here, total_len, KV_HEADS, HEAD_DIM)
    value_heads = values_all.reshape(seqs_here, total_len, KV_HEADS, HEAD_DIM)
    mixed, lse_rows = lax.map(
        lambda blocks: attend(query_pos, blocks), (queries, key_heads, value_heads)
    )
    mixed_b = mixed.reshape(seqs_here, span_len, HEADS * HEAD_DIM).astype(jnp.bfloat16)
    middle = hidden_in + project(mixed_b, w_out)
    ffn_normed, factor_ffn = norm_forward(middle, gain_ffn.astype(jnp.float32))
    ffn_in = ffn_normed.astype(jnp.bfloat16)
    gate_val = project(ffn_in, w_gate)
    up_val = project(ffn_in, w_up)
    inner = (jax.nn.silu(gate_val) * up_val).astype(jnp.bfloat16)
    layer_out = middle + project(inner, w_down)
    kept = (
        hidden_in,
        factor_attn,
        normed_b,
        queries,
        key_heads,
        value_heads,
        lse_rows,
        mixed_b,
        middle,
        factor_ffn,
        ffn_in,
        gate_val,
        up_val,
        inner,
    )
    return (layer_out, kept)


def layer_backward(upstream, kept, weights, cosine, sine, query_pos):
    w_query, w_key, w_value, w_out, w_gate, w_up, w_down, gain_attn, gain_ffn = weights
    (
        hidden_in,
        factor_attn,
        normed_b,
        queries,
        key_heads,
        value_heads,
        lse_rows,
        mixed_b,
        middle,
        factor_ffn,
        ffn_in,
        gate_val,
        up_val,
        inner,
    ) = kept
    seqs_here, span_len, model_width = upstream.shape
    total_len = key_heads.shape[1]
    group_size = HEADS // KV_HEADS
    down_in = upstream.astype(jnp.bfloat16)
    grad_w_down = outer_sum(inner, down_in)
    grad_inner = project_back(down_in, w_down)
    sigma = jax.nn.sigmoid(gate_val)
    grad_gate = (grad_inner * up_val * sigma * (1.0 + gate_val * (1.0 - sigma))).astype(
        jnp.bfloat16
    )
    grad_up = (grad_inner * gate_val * sigma).astype(jnp.bfloat16)
    grad_w_gate = outer_sum(ffn_in, grad_gate)
    grad_w_up = outer_sum(ffn_in, grad_up)
    grad_ffn_in = project_back(grad_gate, w_gate) + project_back(grad_up, w_up)
    grad_norm_ffn, grad_gain_ffn = norm_backward(
        middle, factor_ffn, gain_ffn.astype(jnp.float32), grad_ffn_in
    )
    grad_middle = upstream + grad_norm_ffn
    attn_back = grad_middle.astype(jnp.bfloat16)
    grad_w_out = outer_sum(mixed_b, attn_back)
    grad_mixed = (
        project_back(attn_back, w_out)
        .astype(jnp.bfloat16)
        .reshape(seqs_here, span_len, KV_HEADS, group_size, HEAD_DIM)
    )
    grad_query, grad_key, grad_value = lax.map(
        lambda blocks: attend_back(query_pos, blocks),
        (queries, key_heads, value_heads, lse_rows, grad_mixed),
    )
    key_grad_all = grad_key.reshape(seqs_here, total_len, KV_HEADS * HEAD_DIM)
    value_grad_all = grad_value.reshape(seqs_here, total_len, KV_HEADS * HEAD_DIM)
    key_grad_own, value_grad_own = (
        lax.psum_scatter(
            key_grad_all.astype(jnp.bfloat16), "shard", scatter_dimension=1, tiled=True
        ).astype(jnp.float32),
        lax.psum_scatter(
            value_grad_all.astype(jnp.bfloat16), "shard", scatter_dimension=1, tiled=True
        ).astype(jnp.float32),
    )
    grad_query_pre = rotate_back(
        grad_query.reshape(seqs_here, span_len, HEADS, HEAD_DIM), cosine, sine
    )
    grad_query_pre = grad_query_pre.reshape(seqs_here, span_len, HEADS * HEAD_DIM).astype(
        jnp.bfloat16
    )
    grad_key_pre = rotate_back(
        key_grad_own.reshape(seqs_here, span_len, KV_HEADS, HEAD_DIM), cosine, sine
    )
    grad_key_pre = grad_key_pre.reshape(seqs_here, span_len, KV_HEADS * HEAD_DIM).astype(
        jnp.bfloat16
    )
    grad_value_pre = value_grad_own.astype(jnp.bfloat16)
    grad_w_query = outer_sum(normed_b, grad_query_pre)
    grad_w_key = outer_sum(normed_b, grad_key_pre)
    grad_w_value = outer_sum(normed_b, grad_value_pre)
    grad_normed = (
        project_back(grad_query_pre, w_query)
        + project_back(grad_key_pre, w_key)
        + project_back(grad_value_pre, w_value)
    )
    grad_norm_attn, grad_gain_attn = norm_backward(
        hidden_in, factor_attn, gain_attn.astype(jnp.float32), grad_normed
    )
    grad_hidden = grad_middle + grad_norm_attn
    return (
        grad_hidden,
        (
            grad_w_query,
            grad_w_key,
            grad_w_value,
            grad_w_out,
            grad_w_gate,
            grad_w_up,
            grad_w_down,
            grad_gain_attn,
            grad_gain_ffn,
        ),
    )


def local(
    inputs, out_grad, w_query, w_key, w_value, w_out, w_gate, w_up, w_down, gain_attn, gain_ffn
):
    section_index = lax.axis_index("section")
    shard_index = lax.axis_index("shard")
    micro_count, seqs_here, span_len, model_width = inputs.shape
    query_pos = shard_index * span_len + jnp.arange(span_len, dtype=jnp.int32)
    cosine, sine = rope_tables(query_pos, HEAD_DIM)
    gathered = (
        lax.all_gather(w_query, "shard", axis=1, tiled=True),
        lax.all_gather(w_key, "shard", axis=1, tiled=True),
        lax.all_gather(w_value, "shard", axis=1, tiled=True),
        lax.all_gather(w_out, "shard", axis=1, tiled=True),
        lax.all_gather(w_gate, "shard", axis=1, tiled=True),
        lax.all_gather(w_up, "shard", axis=1, tiled=True),
        lax.all_gather(w_down, "shard", axis=1, tiled=True),
        lax.all_gather(gain_attn, "shard", axis=1, tiled=True),
        lax.all_gather(gain_ffn, "shard", axis=1, tiled=True),
    )
    weights = tuple((gathered_arr[0] for gathered_arr in gathered))
    received = jnp.zeros((seqs_here, span_len, model_width), jnp.bfloat16)
    kept_list = []
    sent_list = []
    for tick_num in range(micro_count + 1):
        own_input = inputs[min(tick_num, micro_count - 1)]
        layer_in = jnp.where(section_index == 0, own_input, received).astype(jnp.float32)
        layer_out, kept = layer_forward(layer_in, weights, cosine, sine, query_pos)
        sent = layer_out.astype(jnp.bfloat16)
        sent_list.append(sent)
        kept_list.append(kept)
        if tick_num < micro_count:
            received = from_behind(sent, "section", 1)
    section_out = jnp.stack(
        [
            jnp.where(section_index == 0, sent_list[micro_idx], sent_list[micro_idx + 1])
            for micro_idx in range(micro_count)
        ]
    )[None]
    regathered = (
        lax.all_gather(w_query, "shard", axis=1, tiled=True),
        lax.all_gather(w_key, "shard", axis=1, tiled=True),
        lax.all_gather(w_value, "shard", axis=1, tiled=True),
        lax.all_gather(w_out, "shard", axis=1, tiled=True),
        lax.all_gather(w_gate, "shard", axis=1, tiled=True),
        lax.all_gather(w_up, "shard", axis=1, tiled=True),
        lax.all_gather(w_down, "shard", axis=1, tiled=True),
        lax.all_gather(gain_attn, "shard", axis=1, tiled=True),
        lax.all_gather(gain_ffn, "shard", axis=1, tiled=True),
    )
    weights = tuple((gathered_arr[0] for gathered_arr in regathered))
    arriving = jnp.zeros((seqs_here, span_len, model_width), jnp.bfloat16)
    totals = None
    grad_list = []
    for tick_num in range(micro_count + 1):
        late_micro = min(max(micro_count - 1 - tick_num, 0), micro_count - 1)
        incoming = jnp.where(section_index == 1, out_grad[late_micro], arriving).astype(jnp.float32)
        micro_now = micro_count - tick_num - section_index
        is_valid = (micro_now >= 0) & (micro_now < micro_count)
        incoming = jnp.where(is_valid, incoming, 0.0)
        grad_hidden, partial_grads = layer_backward(
            incoming, kept_list[micro_count - tick_num], weights, cosine, sine, query_pos
        )
        if totals is None:
            totals = partial_grads
        else:
            totals = jax.tree.map(jnp.add, totals, partial_grads)
        grad_list.append(grad_hidden)
        if tick_num < micro_count:
            arriving = from_behind(grad_hidden.astype(jnp.bfloat16), "section", -1)
    section_grad = jnp.stack(
        [
            jnp.where(
                section_index == 0,
                grad_list[micro_count - micro_idx],
                grad_list[micro_count - 1 - micro_idx],
            )
            for micro_idx in range(micro_count)
        ]
    )[None]
    summed = (
        lax.psum_scatter(
            totals[0][None].astype(jnp.bfloat16), "shard", scatter_dimension=1, tiled=True
        ).astype(jnp.float32),
        lax.psum_scatter(
            totals[1][None].astype(jnp.bfloat16), "shard", scatter_dimension=1, tiled=True
        ).astype(jnp.float32),
        lax.psum_scatter(
            totals[2][None].astype(jnp.bfloat16), "shard", scatter_dimension=1, tiled=True
        ).astype(jnp.float32),
        lax.psum_scatter(
            totals[3][None].astype(jnp.bfloat16), "shard", scatter_dimension=1, tiled=True
        ).astype(jnp.float32),
        lax.psum_scatter(
            totals[4][None].astype(jnp.bfloat16), "shard", scatter_dimension=1, tiled=True
        ).astype(jnp.float32),
        lax.psum_scatter(
            totals[5][None].astype(jnp.bfloat16), "shard", scatter_dimension=1, tiled=True
        ).astype(jnp.float32),
        lax.psum_scatter(
            totals[6][None].astype(jnp.bfloat16), "shard", scatter_dimension=1, tiled=True
        ).astype(jnp.float32),
        lax.psum_scatter(
            totals[7][None].astype(jnp.bfloat16), "shard", scatter_dimension=1, tiled=True
        ).astype(jnp.float32),
        lax.psum_scatter(
            totals[8][None].astype(jnp.bfloat16), "shard", scatter_dimension=1, tiled=True
        ).astype(jnp.float32),
    )
    owned = (
        lax.psum(summed[0].astype(jnp.bfloat16), "replica").astype(jnp.float32),
        lax.psum(summed[1].astype(jnp.bfloat16), "replica").astype(jnp.float32),
        lax.psum(summed[2].astype(jnp.bfloat16), "replica").astype(jnp.float32),
        lax.psum(summed[3].astype(jnp.bfloat16), "replica").astype(jnp.float32),
        lax.psum(summed[4].astype(jnp.bfloat16), "replica").astype(jnp.float32),
        lax.psum(summed[5].astype(jnp.bfloat16), "replica").astype(jnp.float32),
        lax.psum(summed[6].astype(jnp.bfloat16), "replica").astype(jnp.float32),
        lax.psum(summed[7].astype(jnp.bfloat16), "replica").astype(jnp.float32),
        lax.psum(summed[8].astype(jnp.bfloat16), "replica").astype(jnp.float32),
    )
    return (
        section_out,
        section_grad,
        owned[0],
        owned[1],
        owned[2],
        owned[3],
        owned[4],
        owned[5],
        owned[6],
        owned[7],
        owned[8],
    )


def solution(mesh):
    return jax.shard_map(
        local,
        mesh=mesh,
        in_specs=(
            P(None, "replica", "shard", None),
            P(None, "replica", "shard", None),
            P("section", "shard", None),
            P("section", "shard", None),
            P("section", "shard", None),
            P("section", "shard", None),
            P("section", "shard", None),
            P("section", "shard", None),
            P("section", "shard", None),
            P("section", "shard"),
            P("section", "shard"),
        ),
        out_specs=(
            P("section", None, "replica", "shard", None),
            P("section", None, "replica", "shard", None),
            P("section", "shard", None),
            P("section", "shard", None),
            P("section", "shard", None),
            P("section", "shard", None),
            P("section", "shard", None),
            P("section", "shard", None),
            P("section", "shard", None),
            P("section", "shard"),
            P("section", "shard"),
        ),
        check_vma=False,
    )
```

profile of v0, /device:TPU:1, one launch (start us, length us, event | category | flops | bytes accessed | tf_op | source)
XLA Modules:
  0.0 1262.8 jit_solution(9642292796956833925)
XLA Ops:
  12.5 22.9 %all_gather.55 = bf16[1,576,192]{2,0,1:T(2,128)(2,1)S(1)} all-gather(bf16[1,36,192]{2,0,1:T(2,128)(2,1)S(1)} %copy.70), channel_id=1, replica_groups=mesh['section'=2,'shard'=16,'replica'=4] {'shard'}, dimensions={1}, use_global_device_ids=true | all-gather | bytes 235008 | tf_op jit(solution)/shard_map/all_gather | solution.py:280
  40.1 31.3 %all-reduce.13 = (bf16[576]{0:T(1024)(128)(2,1)S(1)}, bf16[576]{0:T(1024)(128)(2,1)S(1)}) all-reduce(bf16[576]{0:T(1024)(128)(2,1)S(1)} %dynamic-update-slice, bf16[576]{0:T(1024)(128)(2,1)S(1)} %dynamic-update-slice.1), channel_id=1, replica_groups=mesh['section'=2,'shard'=16,'replica'=4] {'shard'}, use_global_device_ids=true, to_apply=%add | all-reduce | flops 1152 | bytes 4608
  74.2 21.0 %all-gather = bf16[2048,192]{0,1:T(8,128)(2,1)} all-gather(bf16[128,192]{0,1:T(8,128)(2,1)S(1)} %convolution_convert_fusion.5), channel_id=2, replica_groups=mesh['section'=2,'shard'=16,'replica'=4] {'shard'}, dimensions={0}, use_global_device_ids=true | all-gather | bytes 835584 | tf_op jit(solution)/shard_map/all_gather | solution.py:136
  96.0 21.8 %all_gather.57 = bf16[1,576,192]{2,0,1:T(2,128)(2,1)S(1)} all-gather(bf16[1,36,192]{2,0,1:T(2,128)(2,1)S(1)} %copy.72), channel_id=1, replica_groups=mesh['section'=2,'shard'=16,'replica'=4] {'shard'}, dimensions={1}, use_global_device_ids=true | all-gather | bytes 235008 | tf_op jit(solution)/shard_map/all_gather | solution.py:279
  119.3 20.9 %all-gather.1 = bf16[2048,192]{0,1:T(8,128)(2,1)S(1)} all-gather(bf16[128,192]{0,1:T(8,128)(2,1)S(1)} %fusion.256), channel_id=3, replica_groups=mesh['section'=2,'shard'=16,'replica'=4] {'shard'}, dimensions={0}, use_global_device_ids=true | all-gather | bytes 835584 | tf_op jit(solution)/shard_map/all_gather | solution.py:135
  140.3 21.1 %all_gather.59 = bf16[1,576,576]{2,0,1:T(2,128)(2,1)S(1)} all-gather(bf16[1,36,576]{2,0,1:T(2,128)(2,1)S(1)} %copy.74), channel_id=1, replica_groups=mesh['section'=2,'shard'=16,'replica'=4] {'shard'}, dimensions={1}, use_global_device_ids=true | all-gather | bytes 705024 | tf_op jit(solution)/shard_map/all_gather | solution.py:278
  163.0 21.8 %all_gather.60 = bf16[1,576,576]{2,0,1:T(2,128)(2,1)S(1)} all-gather(bf16[1,36,576]{2,0,1:T(2,128)(2,1)S(1)} %copy.76), channel_id=1, replica_groups=mesh['section'=2,'shard'=16,'replica'=4] {'shard'}, dimensions={1}, use_global_device_ids=true | all-gather | bytes 705024 | tf_op jit(solution)/shard_map/all_gather | solution.py:281
  214.7 17.2 %all-gather.2 = bf16[2048,192]{0,1:T(8,128)(2,1)S(1)} all-gather(bf16[128,192]{0,1:T(8,128)(2,1)S(1)} %convolution_convert_fusion.4), channel_id=4, replica_groups=mesh['section'=2,'shard'=16,'replica'=4] {'shard'}, dimensions={0}, use_global_device_ids=true | all-gather | bytes 835584 | tf_op jit(solution)/shard_map/all_gather | solution.py:136
  232.0 19.6 %all-gather.3 = bf16[2048,192]{0,1:T(8,128)(2,1)S(1)} all-gather(bf16[128,192]{0,1:T(8,128)(2,1)S(1)} %fusion.258), channel_id=5, replica_groups=mesh['section'=2,'shard'=16,'replica'=4] {'shard'}, dimensions={0}, use_global_device_ids=true | all-gather | bytes 835584 | tf_op jit(solution)/shard_map/all_gather | solution.py:135
  263.0 3.7 collective-permute-start.1
  270.8 18.0 %all-gather.4 = bf16[2048,192]{0,1:T(8,128)(2,1)S(1)} all-gather(bf16[128,192]{0,1:T(8,128)(2,1)S(1)} %convolution_convert_fusion.3), channel_id=6, replica_groups=mesh['section'=2,'shard'=16,'replica'=4] {'shard'}, dimensions={0}, use_global_device_ids=true | all-gather | bytes 835584 | tf_op jit(solution)/shard_map/all_gather | solution.py:136
  288.8 19.5 %all-gather.5 = bf16[2048,192]{0,1:T(8,128)(2,1)S(1)} all-gather(bf16[128,192]{0,1:T(8,128)(2,1)S(1)} %fusion.260), channel_id=7, replica_groups=mesh['section'=2,'shard'=16,'replica'=4] {'shard'}, dimensions={0}, use_global_device_ids=true | all-gather | bytes 835584 | tf_op jit(solution)/shard_map/all_gather | solution.py:135
  318.4 5.1 fusion.8
  323.5 10.5 fusion.10
  334.0 4.1 convolution_multiply_fusion.2
  338.1 4.1 fusion.44
  344.7 3.7 copy.123
  351.4 5.9 copy.125
  373.9 105.0 %reduce-scatter.32.cloned.1.call-done = bf16[128,192]{1,0:T(8,128)(2,1)} async-done(((bf16[2048,192]{1,0:T(8,128)(2,1)}), bf16[128,192]{1,0:T(8,128)(2,1)}) %reduce-scatter.32.cloned.1.call-update) | async-done | bytes 49168
  484.4 70.2 %reduce-scatter.34.cloned.1.call-done = bf16[128,192]{1,0:T(8,128)(2,1)} async-done(((bf16[2048,192]{1,0:T(8,128)(2,1)}), bf16[128,192]{1,0:T(8,128)(2,1)}) %reduce-scatter.34.cloned.1.call-update) | async-done | bytes 49168
  573.5 5.2 fusion.5
  578.7 10.4 fusion.7
  589.1 3.9 fusion.45
  593.1 3.8 copy.127
  602.0 6.2 fusion.50
  608.2 5.9 copy.129
  626.4 46.9 %reduce-scatter.36.cloned.1.call-done = bf16[128,192]{1,0:T(8,128)(2,1)} async-done(((bf16[2048,192]{1,0:T(8,128)(2,1)}), bf16[128,192]{1,0:T(8,128)(2,1)}) %reduce-scatter.36.cloned.1.call-update) | async-done | bytes 49168
  678.8 70.3 %reduce-scatter.38.cloned.1.call-done = bf16[128,192]{1,0:T(8,128)(2,1)} async-done(((bf16[2048,192]{1,0:T(8,128)(2,1)}), bf16[128,192]{1,0:T(8,128)(2,1)}) %reduce-scatter.38.cloned.1.call-update) | async-done | bytes 49168
  767.9 4.7 fusion.2
  772.5 10.5 fusion.4
  783.0 4.8 fusion.46
  787.9 4.6 copy.131
  798.0 6.2 fusion.47
  804.3 4.6 copy.133
  821.0 46.2 %reduce-scatter.40.cloned.1.call-done = bf16[128,192]{1,0:T(8,128)(2,1)} async-done(((bf16[2048,192]{1,0:T(8,128)(2,1)}), bf16[128,192]{1,0:T(8,128)(2,1)}) %reduce-scatter.40.cloned.1.call-update) | async-done | bytes 49168
  868.3 74.7 %reduce-scatter.42.cloned.1.call-done = bf16[128,192]{1,0:T(8,128)(2,1)} async-done(((bf16[2048,192]{1,0:T(8,128)(2,1)}), bf16[128,192]{1,0:T(8,128)(2,1)}) %reduce-scatter.42.cloned.1.call-update) | async-done | bytes 49168
  955.3 6.0 copy.143
  961.3 3.9 copy.167
  968.1 5.0 fusion.30
  973.1 59.0 %fusion.321 = (bf16[48,1536]{1,0:T(8,128)(2,1)}, bf16[48,1536]{1,0:T(8,128)(2,1)}) fusion(bf16[1,576,1536]{2,1,0:T(8,128)(2,1)S(1)} %fusion.29, bf16[1,576,1536]{2,1,0:T(8,128)(2,1)} %fusion.30), kind=kCustom, calls=%all-reduce-scatter.2 | all-reduce-scatter fusion | flops 2359297 | bytes 3834368
  1046.2 5.0 collective-permute-start.10
  1054.4 3.7 collective-permute-start.8
  1060.1 4.3 concatenate.141
  1064.4 8.1 concatenate.142
  1077.7 33.2 %all-reduce.12 = (bf16[1,576]{1,0:T(2,128)(2,1)S(1)}, bf16[1,576]{1,0:T(2,128)(2,1)S(1)}) all-reduce(bf16[1,576]{1,0:T(2,128)(2,1)S(1)} %convert_element_type.831, bf16[1,576]{1,0:T(2,128)(2,1)S(1)} %convert_element_type.834), channel_id=21, replica_groups=mesh['section'=2,'shard'=16,'replica'=4] {'shard'}, use_global_device_ids=true, to_apply=%region_44.45.clone | all-reduce | flops 1152 | bytes 4608
  1114.5 45.2 %reduce-scatter.44.cloned.1.call-done = bf16[96,576]{1,0:T(8,128)(2,1)} async-done(((bf16[1536,576]{1,0:T(8,128)(2,1)}), bf16[96,576]{1,0:T(8,128)(2,1)}) %reduce-scatter.44.cloned.1.call-update) | async-done | bytes 110608
  1163.5 42.8 %all-reduce.24.cloned.1.call-done = (bf16[1,36,576]{2,1,0:T(8,128)(2,1)}, bf16[1,36,576]{2,1,0:T(8,128)(2,1)}, bf16[1,36,192]{2,0,1:T(2,128)(2,1)}, bf16[1,36,19...) async-done(((bf16[1,36,576]{2,1,0:T(8,128)(2,1)}, bf16[1,36,576]{2,1,0:T(8,128)(2,1)}, bf16[1,36,192]{2,0,1:T(2,128)(2,1)}, ...) | async-done | bytes 110752 | tf_op jit(solution)/shard_map/psum | solution.py:378
  1214.4 36.2 %all-reduce.26.cloned.1.call-done = (bf16[1,36,1536]{2,1,0:T(8,128)(2,1)}, bf16[1,36,1536]{2,1,0:T(8,128)(2,1)}, bf16[1,96,576]{1,2,0:T(8,128)(2,1)}) async-done(((bf16[1,36,1536]{2,1,0:T(8,128)(2,1)}, bf16[1,36,1536]{2,1,0:T(8,128)(2,1)}, bf16[1,96,576]{1,2,0:T(8,128)(2,1)}), (bf16[1,36,1536]{2,1,0:T(8,128)(2,1)}, bf16[1,36,1536]{2,1,0:T(8,128)(2,1)}, ...) | async-done | bytes 331792 | tf_op jit(solution)/shard_map/psum | solution.py:382
  (602 shorter events, 235.4 us)
Async XLA Ops:
  7.2 111.5 %copy-start.29 = (bf16[2,1,128,576]{2,3,1,0:T(8,128)(2,1)S(1)}, bf16[2,1,128,576]{2,3,1,0:T(8,128)(2,1)}, u32[]{:S(2)}) copy-start(bf16[2,1,128,576]{2,3,1,0:T(8,128)(2,1)} %param.11) | copy-start | bytes 884740
  7.2 133.0 %copy-start.143 = (bf16[1,36,576]{2,1,0:T(8,128)(2,1)S(1)}, bf16[1,36,576]{2,1,0:T(8,128)(2,1)}, u32[]{:S(2)}) copy-start(bf16[1,36,576]{2,1,0:T(8,128)(2,1)} %param.13) | copy-start | bytes 124420
  7.2 189.6 %all-gather.10.cloned.1.call-start = ((), (), s32[]{:S(2)}) async-start(), calls=%async_computation.7 | async-start | bytes 3760128 | tf_op jit(solution)/shard_map/all_gather | solution.py:282
  9.1 190.2 %all-gather.12.cloned.1.call-start = ((), (), s32[]{:S(2)}) async-start(), calls=%async_computation.8 | async-start | bytes 3760128 | tf_op jit(solution)/shard_map/all_gather | solution.py:283
  10.9 194.5 %all-gather.14.cloned.1.call-start = ((), (), s32[]{:S(2)}) async-start(), calls=%async_computation.9 | async-start | bytes 2088960 | tf_op jit(solution)/shard_map/all_gather | solution.py:284
  11.6 467.2 %reduce-scatter.32.cloned.1.call-start = ((), (), s32[]{:S(2)}) async-start(), calls=%async_computation.10 | async-start | bytes 1114112
  71.4 90.1 %copy-start.77 = (f32[576]{0:T(1024)}, f32[576]{0:T(1024)S(1)}, u32[]{:S(2)}) copy-start(f32[576]{0:T(1024)S(1)} %convert_element_type.839) | copy-start | bytes 6916
  73.0 89.1 %copy-start.150 = (f32[128]{0:T(128)}, f32[128]{0:T(128)S(1)}, u32[]{:S(2)}) copy-start(f32[128]{0:T(128)S(1)} %get-tuple-element.275) | copy-start | bytes 1540
  119.2 67.1 %copy-start.43 = (f32[128,64]{0,1:T(8,128)}, f32[128,64]{0,1:T(8,128)S(1)}, u32[]{:S(2)}) copy-start(f32[128,64]{0,1:T(8,128)S(1)} %get-tuple-element.269) | copy-start | bytes 98308
  184.9 133.1 %copy-start.8 = (bf16[1,576,576]{2,1,0:T(8,128)(2,1)}, bf16[1,576,576]{2,1,0:T(8,128)(2,1)S(1)}, u32[]{:S(2)}) copy-start(bf16[1,576,576]{2,1,0:T(8,128)(2,1)S(1)} %copy.150) | copy-start | bytes 1990660
  208.0 4.8 collective-permute-start
  263.0 5.8 collective-permute-start.1
  351.3 203.3 %reduce-scatter.34.cloned.1.call-start = ((), (), s32[]{:S(2)}) async-start(), calls=%async_computation.11 | async-start | bytes 1114112
  365.8 307.5 %reduce-scatter.36.cloned.1.call-start = ((), (), s32[]{:S(2)}) async-start(), calls=%async_computation.12 | async-start | bytes 1114112
  370.4 203.1 %slice-start.3 = ((s8[9437184]{0:T(1024)(128)(4,1)}), s8[1048576]{0:T(1024)(128)(4,1)S(1)}, s32[]{:S(2)}) async-start(s8[9437184]{0:T(1024)(128)(4,1)} %bitcast.771), calls=%async_computation.23 | async-start | bytes 2097152
  563.3 6.2 collective-permute-start.2
  599.6 149.5 %reduce-scatter.38.cloned.1.call-start = ((), (), s32[]{:S(2)}) async-start(), calls=%async_computation.13 | async-start | bytes 1114112
  620.9 246.2 %reduce-scatter.40.cloned.1.call-start = ((), (), s32[]{:S(2)}) async-start(), calls=%async_computation.14 | async-start | bytes 1114112
  623.8 144.0 %slice-start = ((s8[9437184]{0:T(1024)(128)(4,1)}), s8[1048576]{0:T(1024)(128)(4,1)S(1)}, s32[]{:S(2)}) async-start(s8[9437184]{0:T(1024)(128)(4,1)} %bitcast.769), calls=%async_computation.20 | async-start | bytes 2097152
  757.9 6.3 collective-permute-start.3
  793.6 149.4 %reduce-scatter.42.cloned.1.call-start = ((), (), s32[]{:S(2)}) async-start(), calls=%async_computation.15 | async-start | bytes 1114112
  814.3 297.2 %all-reduce.22.cloned.1.call-start = ((), (), s32[]{:S(2)}) async-start(), calls=%async_computation.17 | async-start | bytes 5308416
  815.5 128.4 %copy-start.107 = (bf16[1,128,9,64]{1,3,2,0:T(8,128)(2,1)}, bf16[1,128,9,64]{1,3,2,0:T(8,128)(2,1)S(1)}, u32[]{:S(2)}) copy-start(bf16[1,128,9,64]{1,3,2,0:T(8,128)(2,1)S(1)} %fusion.204) | copy-start | bytes 442372
  818.8 128.0 %copy-start.73 = (f32[576,192]{0,1:T(8,128)S(1)}, f32[576,192]{0,1:T(8,128)}, u32[]{:S(2)}) copy-start(f32[576,192]{0,1:T(8,128)} %convolution_add_fusion.1) | copy-start | bytes 1327108
  820.9 127.9 %copy-start.68 = (bf16[128,576]{0,1:T(8,128)(2,1)S(1)}, bf16[128,576]{0,1:T(8,128)(2,1)}, u32[]{:S(2)}) copy-start(bf16[128,576]{0,1:T(8,128)(2,1)} %copy-done.67) | copy-start | bytes 442372
  820.9 127.9 %copy-start.94 = (bf16[128,1536]{1,0:T(8,128)(2,1)S(1)}, bf16[128,1536]{1,0:T(8,128)(2,1)}, u32[]{:S(2)}) copy-start(bf16[128,1536]{1,0:T(8,128)(2,1)} %copy-done.93) | copy-start | bytes 1179652
  868.3 75.8 %copy-start.129 = (bf16[1,128,192]{1,2,0:T(8,128)(2,1)}, bf16[1,128,192]{1,2,0:T(8,128)(2,1)S(1)}, u32[]{:S(2)}) copy-start(bf16[1,128,192]{1,2,0:T(8,128)(2,1)S(1)} %fusion.266) | copy-start | bytes 147460
  948.5 211.3 %reduce-scatter.44.cloned.1.call-start = ((), (), s32[]{:S(2)}) async-start(), calls=%async_computation.16 | async-start | bytes 2088960
  968.0 238.3 %all-reduce.24.cloned.1.call-start = ((), (), s32[]{:S(2)}) async-start(), calls=%async_computation.18 | async-start | bytes 354304 | tf_op jit(solution)/shard_map/psum | solution.py:378
  973.1 86.9 %copy-start.152 = (f32[576]{0:T(1024)S(1)}, f32[576]{0:T(1024)}, u32[]{:S(2)}) copy-start(f32[576]{0:T(1024)} %get-tuple-element.189) | copy-start | bytes 6916
  973.1 86.9 %copy-start.153 = (f32[576]{0:T(1024)S(1)}, f32[576]{0:T(1024)}, u32[]{:S(2)}) copy-start(f32[576]{0:T(1024)} %get-tuple-element.187) | copy-start | bytes 6916
  973.1 86.9 %copy-start.154 = (f32[576]{0:T(1024)S(1)}, f32[576]{0:T(1024)}, u32[]{:S(2)}) copy-start(f32[576]{0:T(1024)} %get-tuple-element.191) | copy-start | bytes 6916
  973.1 101.7 %copy-start.24 = (bf16[1,576,192]{1,2,0:T(8,128)(2,1)S(1)}, bf16[1,576,192]{1,2,0:T(8,128)(2,1)}, u32[]{:S(2)}) copy-start(bf16[1,576,192]{1,2,0:T(8,128)(2,1)} %copy-done.22) | copy-start | bytes 663556
  973.1 102.8 %copy-start.82 = (f32[576]{0:T(1024)S(1)}, f32[576]{0:T(1024)}, u32[]{:S(2)}) copy-start(f32[576]{0:T(1024)} %copy-done.77) | copy-start | bytes 6916
  1032.1 129.6 %copy-start.17 = (bf16[1,128,576]{1,2,0:T(8,128)(2,1)S(1)}, bf16[1,128,576]{1,2,0:T(8,128)(2,1)}, u32[]{:S(2)}) copy-start(bf16[1,128,576]{1,2,0:T(8,128)(2,1)} %copy-done.14) | copy-start | bytes 442372
  1032.1 129.6 %copy-start.28 = (f32[1,128,576]{1,2,0:T(8,128)S(1)}, f32[1,128,576]{1,2,0:T(8,128)}, u32[]{:S(2)}) copy-start(f32[1,128,576]{1,2,0:T(8,128)} %copy-done.26) | copy-start | bytes 884740
  1032.1 129.6 %copy-start.54 = (f32[1,128,576]{1,2,0:T(8,128)S(1)}, f32[1,128,576]{1,2,0:T(8,128)}, u32[]{:S(2)}) copy-start(f32[1,128,576]{1,2,0:T(8,128)} %copy-done.53) | copy-start | bytes 884740
  1032.1 129.6 %copy-start.64 = (f32[128,576]{0,1:T(8,128)S(1)}, f32[128,576]{0,1:T(8,128)}, u32[]{:S(2)}) copy-start(f32[128,576]{0,1:T(8,128)} %copy-done.63) | copy-start | bytes 884740
  1032.1 129.6 %copy-start.116 = (f32[1,128,576]{1,2,0:T(8,128)S(1)}, f32[1,128,576]{1,2,0:T(8,128)}, u32[]{:S(2)}) copy-start(f32[1,128,576]{1,2,0:T(8,128)} %get-tuple-element.231) | copy-start | bytes 884740
  1033.2 21.2 %collective-permute-start.6 = (bf16[48,1536]{1,0:T(8,128)(2,1)}, bf16[48,1536]{1,0:T(8,128)(2,1)S(1)}, u32[]{:S(2)}, u32[]{:S(2)}) collective-permute-start(bf16[48,1536]{1,0:T(8,128)(2,1)} %get-tuple-element.228), channel_id=1, source_target_pairs={{0,12},{4,16},{8,20},{12,24},{16,28},{20,32},{24,36},{28,40},{32,4... | collective-permute-start | bytes 442376
  1034.5 23.6 %collective-permute-start.5 = (bf16[48,1536]{1,0:T(8,128)(2,1)}, bf16[48,1536]{1,0:T(8,128)(2,1)S(1)}, u32[]{:S(2)}, u32[]{:S(2)}) collective-permute-start(bf16[48,1536]{1,0:T(8,128)(2,1)} %get-tuple-element.228), channel_id=1, source_target_pairs={{0,8},{4,12},{8,16},{12,20},{16,24},{20,28},{24,32},{28,36},{32,40... | collective-permute-start | bytes 442376
  1037.2 14.0 %collective-permute-start.7 = (bf16[36,1536]{1,0:T(8,128)(2,1)S(1)}, bf16[36,1536]{1,0:T(8,128)(2,1)S(1)}, u32[]{:S(2)}, u32[]{:S(2)}) collective-permute-start(bf16[36,1536]{1,0:T(8,128)(2,1)S(1)} %slice.138), channel_id=1, source_target_pairs={{0,16},{4,20},{8,24},{12,28},{16,32},{20,36},{24,40},{28,44},{32,4... | collective-permute-start | bytes 331784
  1041.6 18.5 %collective-permute-start.4 = (bf16[48,1536]{1,0:T(8,128)(2,1)}, bf16[48,1536]{1,0:T(8,128)(2,1)}, u32[]{:S(2)}, u32[]{:S(2)}) collective-permute-start(bf16[48,1536]{1,0:T(8,128)(2,1)} %get-tuple-element.228), channel_id=1, source_target_pairs={{0,4},{4,8},{8,12},{12,16},{16,20},{20,24},{24,28},{28,32},{32,36}... | collective-permute-start | bytes 442376
  1046.2 18.2 %collective-permute-start.10 = (bf16[48,1536]{1,0:T(8,128)(2,1)}, bf16[48,1536]{1,0:T(8,128)(2,1)S(1)}, u32[]{:S(2)}, u32[]{:S(2)}) collective-permute-start(bf16[48,1536]{1,0:T(8,128)(2,1)} %get-tuple-element.229), channel_id=1, source_target_pairs={{0,12},{4,16},{8,20},{12,24},{16,28},{20,32},{24,36},{28,40},{32,4... | collective-permute-start | bytes 442376
  1051.2 13.2 %collective-permute-start.9 = (bf16[48,1536]{1,0:T(8,128)(2,1)}, bf16[48,1536]{1,0:T(8,128)(2,1)}, u32[]{:S(2)}, u32[]{:S(2)}) collective-permute-start(bf16[48,1536]{1,0:T(8,128)(2,1)} %get-tuple-element.229), channel_id=1, source_target_pairs={{0,8},{4,12},{8,16},{12,20},{16,24},{20,28},{24,32},{28,36},{32,40... | collective-permute-start | bytes 442376
  1054.4 10.1 collective-permute-start.8
  1058.1 6.3 collective-permute-start.11
  1114.5 136.1 %all-reduce.26.cloned.1.call-start = ((), (), s32[]{:S(2)}) async-start(), calls=%async_computation.19 | async-start | bytes 786432 | tf_op jit(solution)/shard_map/psum | solution.py:382
  (147 other events, 1434.7 us)
Sparse Core Ops, SparseCore 0:
  10.7 53.0 all-gather.9
  66.5 50.9 all-gather.11
  119.6 46.8 all-gather.13
  351.4 127.4 reduce-scatter.31
  482.3 72.2 reduce-scatter.33
  599.8 73.4 reduce-scatter.35
  676.8 72.2 reduce-scatter.37
  793.8 73.3 reduce-scatter.39
  870.7 72.2 reduce-scatter.41
  948.6 134.3 all-reduce.21
  1086.6 73.0 reduce-scatter.43
  1163.7 42.5 all-reduce.23
  1209.8 40.7 all-reduce.25
where the time goes:
time: 1270 us; the launch traced here: 1260 us
  waiting for transfers between devices  542 us (43%)
  blocking collectives  327 us (26%)
  matrix products  150 us (12%)
  local copies, waits for them, and re-layouts  126 us (10%)
  other arithmetic  64 us (5%)
  starting transfers between devices  34.3 us (3%)
  between operations  18.9 us (1%)
    unnamed x29, waiting for transfers between devices  459 us
    unnamed x3, blocking collectives  123 us
    unnamed x397, local copies, waits for them, and re-layouts  121 us
    all_gather x3, blocking collectives, layer_forward(): lax.all_gather(keys_local, 'shard', axis=1, tiled=True)  60 us
    all_gather x3, blocking collectives, layer_forward(): lax.all_gather(values_local, 'shard', axis=1, tiled=True)  56.2 us
    dot_general x21, matrix products, outer_sum(): jnp.einsum('scd,sce->de', left, right, preferred_element_type=jnp.float32)  45 us
    psum x1, waiting for transfers between devices, local(): lax.psum(summed[0].astype(jnp.bfloat16), 'replica').astype(jnp.float32)  42.8 us
    psum x1, waiting for transfers between devices, local(): lax.psum(summed[4].astype(jnp.bfloat16), 'replica').astype(jnp.float32)  36.2 us
  transfers between devices with their start and end apart: 25, of which 12 were waited for; matrix products, arithmetic and copies ran while one was open for 19% of the time, Pallas kernels for 0%

commit v1 on v0

v1 whole, which is shorter than its diff:
```python
import functools

import jax
import jax.numpy as jnp
from jax import lax
from jax.experimental import pallas as pl
from jax.experimental.pallas import tpu as pltpu
from jax.sharding import PartitionSpec as P

HEADS = 9
KV_HEADS = 3
HEAD_DIM = 64
D = 576
FF = 1536
TOK = 128
SHARDS = 16
SIDE = 4
ROWS = 36
PAD = 48
BAND = SIDE * ROWS
FROWS = 96
FBAND = SIDE * FROWS
GU = 2 * FF
QO = 1664
QKV = 1024
OAT = 1024
CHUNK = 512
GROUP = 3 * TOK

bf16 = jnp.bfloat16
f32 = jnp.float32
MESH = pl.DeviceIdType.MESH
epsilon = 1e-05
rope_base = 100000.0
score_scale = 0.125


def dot(a, b):
    return lax.dot_general(a, b, (((1,), (0,)), ((), ())), preferred_element_type=f32)


def dot_nt(a, b):
    return lax.dot_general(a, b, (((1,), (1,)), ((), ())), preferred_element_type=f32)


def dot_tn(a, b):
    return lax.dot_general(a, b, (((0,), (0,)), ((), ())), preferred_element_type=f32)


def factor_of(v):
    return lax.rsqrt(jnp.mean(v * v, axis=-1, keepdims=True) + epsilon)


def norm_back(v, r, gain, up):
    scaled = gain * up
    return r * scaled - v * (r * r * r) * jnp.mean(scaled * v, axis=-1, keepdims=True)


def half_swap(u):
    width = u.shape[1]
    lane = lax.broadcasted_iota(jnp.int32, u.shape, 1)
    first = lax.rem(lane, HEAD_DIM) < HEAD_DIM // 2
    return jnp.where(first, pltpu.roll(u, width - 32, 1), pltpu.roll(u, 32, 1))


def body(
    x_ref, dy_ref, p0_ref, p1_ref, pd_ref, cos_ref, sin_ref,
    out_ref, dx_ref, gq_ref, gk_ref, gv_ref, go_ref, gg_ref, gu_ref, gd_ref, gain_ref,
    stage, w_gu, w_qo, w_d, kv, dkv_s, dkv_r, scr, mx, acc,
    xs_, a_, q8_, o_, lse_, mid_, bn_, gu_, hid_,
    dyb_, dob_, delta_, dq_, dkv_acc, acc2, gain_term,
    g_gu, g_qo, g_d, zr, zr_d, ys, ys_d, yr, yr_d, xs, xs_d, xr, xr_d, fs, fs_d, fr, fr_d,
    osend, orecv, dsend, drecv,
    ssem, rsem, credit,
):
    sec = lax.axis_index("section")
    sh = lax.axis_index("shard")
    rep = lax.axis_index("replica")
    z, y = lax.div(sh, SIDE), lax.rem(sh, SIDE)
    core = lax.rem(rep, 2)
    sib = rep + 1 - 2 * core
    far = lax.rem(rep + 2, 4)
    used = [0]

    def take(n):
        at = used[0]
        used[0] += n
        return at

    def copy(src, dst, at, **dev):
        return pltpu.make_async_remote_copy(
            src_ref=src, dst_ref=dst, send_sem=ssem.at[at], recv_sem=rsem.at[at],
            device_id=dev, device_id_type=MESH,
        )

    def arrived(dst, at):
        copy(dst, dst, at, shard=sh).wait_recv()

    def sent(src, at):
        copy(src, src, at, shard=sh).wait_send()

    def y_peer(d):
        return z * SIDE + lax.rem(y + d, SIDE)

    def z_peer(d):
        return lax.rem(z + d, SIDE) * SIDE + y

    def z_from(d):
        return lax.rem(z + SIDE - d, SIDE)

    def y_from(d):
        return lax.rem(y + SIDE - d, SIDE)

    kv[...] = jnp.zeros_like(kv)
    ys[...] = jnp.zeros_like(ys)
    barrier = pltpu.get_barrier_semaphore()

    def greet(d, c):
        pl.semaphore_signal(barrier, inc=1, device_id={"shard": lax.rem(sh + d, SHARDS)}, device_id_type=MESH)
        return c

    lax.fori_loop(1, SHARDS, greet, 0)
    pl.semaphore_signal(barrier, inc=1, device_id={"replica": sib}, device_id_type=MESH)
    pl.semaphore_signal(barrier, inc=1, device_id={"replica": far}, device_id_type=MESH)
    pl.semaphore_signal(barrier, inc=1, device_id={"section": 1 - sec}, device_id_type=MESH)
    pl.semaphore_signal(barrier, inc=1, device_id={"section": 1 - sec, "replica": far}, device_id_type=MESH)
    pl.semaphore_wait(barrier, SHARDS - 1 + 4)

    packs = ((0, p0_ref, w_gu, GU), (1, p1_ref, w_qo, QO))
    at_x, at_xd = take(1), take(1)
    at_y = [take(3) for _ in range(2)]
    at_z = [take(3) for _ in range(2)]
    at_f = [take(4) for _ in range(2)]
    at_dz = [take(3) for _ in range(2)]
    at_dy = [take(3) for _ in range(2)]
    at_df = [take(1) for _ in range(2)]

    def x_start():
        for c, p, w, width in packs:
            @pl.when(core == c)
            def _():
                copy(p, stage.at[sec, y, :, pl.ds(0, width)], at_x, section=1 - sec).start()
                stage[sec, y, :, 0:width] = p[...]

        @pl.when(core == 1)
        def _():
            copy(pd_ref, w_d.at[sec, z, y], at_xd, section=1 - sec).start()
            w_d[sec, z, y] = pd_ref[...]

    def y_start(l):
        for c, p, w, width in packs:
            @pl.when(core == c)
            def _():
                own = stage.at[l, y, :, pl.ds(0, width)]

                @pl.when(sec != l)
                def _():
                    arrived(own, at_x)

                for d in range(1, SIDE):
                    copy(own, own, at_y[l] + d - 1, shard=y_peer(d)).start()

    def dz_start(l):
        @pl.when(core == 1)
        def _():
            own = w_d.at[l, z, y]

            @pl.when(sec != l)
            def _():
                arrived(own, at_xd)

            for d in range(1, SIDE):
                copy(own, own, at_dz[l] + d - 1, shard=z_peer(d)).start()

    def z_start(l):
        for c, p, w, width in packs:
            @pl.when(core == c)
            def _():
                for d in range(1, SIDE):
                    arrived(stage.at[l, y_from(d), :, pl.ds(0, width)], at_y[l] + d - 1)
                for at in range(0, width, 128):
                    cols = pl.ds(at, 128)
                    parts = [stage[l, j, :, cols][0:ROWS].astype(f32) for j in range(SIDE)]
                    w[l, z, :, cols] = jnp.concatenate(parts, axis=0).astype(bf16)
                own = w.at[l, z]
                for d in range(1, SIDE):
                    copy(own, own, at_z[l] + d - 1, shard=z_peer(d)).start()
                copy(own, own, at_f[l], replica=sib).start()

    def dy_start(l):
        @pl.when(core == 1)
        def _():
            for d in range(1, SIDE):
                arrived(w_d.at[l, z_from(d), y], at_dz[l] + d - 1)
            own = w_d.at[l, :, y]
            for d in range(1, SIDE):
                copy(own, own, at_dy[l] + d - 1, shard=y_peer(d)).start()

    def forward_on(l):
        for c, p, w, width in packs:
            @pl.when(core == c)
            def _():
                for d in range(1, SIDE):
                    got = w.at[l, z_from(d)]
                    arrived(got, at_z[l] + d - 1)
                    copy(got, got, at_f[l] + d, replica=sib).start()

    def d_forward_on(l):
        @pl.when(core == 1)
        def _():
            for d in range(1, SIDE):
                arrived(w_d.at[l, :, y_from(d)], at_dy[l] + d - 1)
            copy(w_d.at[l], w_d.at[l], at_df[l], replica=sib).start()

    def gather_end(l):
        for c, p, w, width in packs:
            @pl.when(core != c)
            def _():
                arrived(w.at[l, z], at_f[l])
                for d in range(1, SIDE):
                    arrived(w.at[l, z_from(d)], at_f[l] + d)

        @pl.when(core == 0)
        def _():
            arrived(w_d.at[l], at_df[l])

    def gather_sent(l):
        for c, p, w, width in packs:
            @pl.when(core == c)
            def _():
                own = stage.at[l, y, :, pl.ds(0, width)]

                @pl.when(sec == l)
                def _():
                    sent(p, at_x)

                for d in range(1, SIDE):
                    sent(own, at_y[l] + d - 1)
                    sent(w.at[l, z], at_z[l] + d - 1)
                    sent(w.at[l, z], at_f[l] + d)
                sent(w.at[l, z], at_f[l])

        @pl.when(core == 1)
        def _():
            @pl.when(sec == l)
            def _():
                sent(pd_ref, at_xd)

            for d in range(1, SIDE):
                sent(w_d.at[l, z, y], at_dz[l] + d - 1)
                sent(w_d.at[l, :, y], at_dy[l] + d - 1)
            sent(w_d.at[l], at_df[l])

    at_kv = [take(SHARDS) for _ in range(2)]
    at_dkv = [take(SHARDS) for _ in range(2)]
    tokens = pl.ds(pl.multiple_of(sh * TOK, TOK), TOK)

    def kv_start(l):
        own = kv.at[l, tokens]

        def go(d, c):
            copy(own, own, at_kv[l] + d, shard=sh + d).start()
            return c

        lax.fori_loop(1, SHARDS - sh, go, 0)

    def kv_wait(l):
        def go(d, c):
            arrived(kv.at[l, pl.ds(pl.multiple_of((sh - d) * TOK, TOK), TOK)], at_kv[l] + d)
            return c

        lax.fori_loop(1, sh + 1, go, 0)

    def kv_sent(l):
        def go(d, c):
            sent(kv.at[l, tokens], at_kv[l] + d)
            return c

        lax.fori_loop(1, SHARDS - sh, go, 0)

    def dkv_start(l, j):
        src = dkv_s.at[pl.ds(pl.multiple_of(j * TOK, TOK), TOK)]
        copy(src, dkv_r.at[l, sh - j], at_dkv[l] + sh - j, shard=j).start()

    def dkv_sent(l):
        def go(d, c):
            sent(dkv_s.at[pl.ds(0, TOK)], at_dkv[l] + d)
            return c

        lax.fori_loop(1, sh + 1, go, 0)

    def gains(l):
        tile = w_qo[l, :, :, 896:1024].reshape(D, 128)
        row = lax.broadcasted_iota(jnp.int32, (8, 128), 0)
        lane = lax.broadcasted_iota(jnp.int32, (8, 128), 1)
        pick = jnp.where(lane == row + 64, 1.0, 0.0).astype(bf16)
        both = dot_nt(pick, tile)
        return both[0:1], both[1:2]

    nfull = lax.div(sh, SIDE)

    def causal():
        row = lax.broadcasted_iota(jnp.int32, (GROUP, CHUNK), 0)
        col = lax.broadcasted_iota(jnp.int32, (GROUP, CHUNK), 1)
        return col <= lax.rem(sh, SIDE) * TOK + lax.rem(row, TOK)

    def keys_at(c):
        return pl.ds(pl.multiple_of(c * CHUNK, CHUNK), CHUNK)

    def tables():
        cos = jnp.concatenate([cos_ref[...]] * 6, axis=1)
        sin = jnp.concatenate([sin_ref[...]] * 6, axis=1)
        return cos, sin

    def project_in(l):
        x = xs_[l]
        gain, _ = gains(l)
        a = (x * factor_of(x) * gain).astype(bf16)
        a_[l] = a
        qkv = dot(a, w_qo[l, :, :, 0:QKV].reshape(D, QKV))
        cos, sin = tables()
        u = qkv[:, 0:768]
        turned = u * cos + half_swap(u) * sin
        for h in range(HEADS):
            head = turned[:, h * 64 : h * 64 + 64].astype(bf16)
            q8_[l, h] = (head.astype(f32) * score_scale).astype(bf16)
        block = jnp.concatenate([turned[:, 576:768], qkv[:, 768:960]], axis=1).astype(bf16)
        kv[l, tokens] = block

    def attend(l):
        for g in range(KV_HEADS):
            q = q8_[l, 3 * g : 3 * g + 3].reshape(GROUP, 64)

            def keep(c, s):
                scr[:, keys_at(c)] = s
                top = jnp.maximum(
                    jnp.maximum(s[:, 0:128], s[:, 128:256]), jnp.maximum(s[:, 256:384], s[:, 384:512])
                )
                mx[...] = jnp.maximum(mx[...], top)

            def scores(c):
                k = kv[l, keys_at(c), :][:, g * 64 : g * 64 + 64]
                return dot_nt(q, k)

            mx[...] = jnp.full_like(mx, -1e30)

            def first(c, carry):
                keep(c, scores(c))
                return carry

            lax.fori_loop(0, nfull, first, 0)
            keep(nfull, jnp.where(causal(), scores(nfull), -1e30))
            peak = jnp.max(mx[...], axis=1, keepdims=True)
            acc[...] = jnp.zeros_like(acc)

            def second(c, carry):
                p = jnp.exp(scr[:, keys_at(c)] - peak).astype(bf16)
                v = kv[l, keys_at(c), :][:, 192 + g * 64 : 256 + g * 64]
                v = jnp.concatenate([v, jnp.ones_like(v)], axis=1)
                acc[...] += dot(p, v)
                return carry

            lax.fori_loop(0, nfull + 1, second, 0)
            total = acc[:, 64:65]
            mixed = (acc[:, 0:64] / total).astype(bf16)
            lse_[l, g] = peak + jnp.log(total)
            o_[l, 3 * g : 3 * g + 3] = mixed.reshape(3, TOK, 64)

    def heads_in(ref):
        return jnp.concatenate([ref[h] for h in range(HEADS)], axis=1)

    def after_attention(l):
        o = heads_in(o_.at[l])
        mid = xs_[l] + dot(o, w_qo[l, :, :, OAT : OAT + D].reshape(D, D))
        mid_[l] = mid
        _, gain = gains(l)
        bn_[l] = (mid * factor_of(mid) * gain).astype(bf16)
        acc2[...] = mid

        def tile(t, c):
            gcols = pl.ds(pl.multiple_of(t * FBAND, 128), FBAND)
            ucols = pl.ds(pl.multiple_of(FF + t * FBAND, 128), FBAND)
            bn = bn_[l]
            gt = dot(bn, w_gu[l, :, :, gcols].reshape(D, FBAND))
            up = dot(bn, w_gu[l, :, :, ucols].reshape(D, FBAND))
            gu_[l, :, gcols] = gt
            gu_[l, :, ucols] = up
            hid = (gt * jax.nn.sigmoid(gt) * up).astype(bf16)
            hid_[l, :, gcols] = hid
            acc2[...] += dot(hid, w_d[l, t].reshape(FBAND, D))
            return c

        lax.fori_loop(0, SIDE, tile, 0)
        return acc2[...]

    def ffn_back(l, dy):
        dyb_[...] = dy.astype(bf16)
        acc2[...] = jnp.zeros_like(acc2)

        def tile(t, c):
            gcols = pl.ds(pl.multiple_of(t * FBAND, 128), FBAND)
            ucols = pl.ds(pl.multiple_of(FF + t * FBAND, 128), FBAND)
            dyb = dyb_[...]
            bn = bn_[l]
            wd = w_d[l, t].reshape(FBAND, D)
            dhid = dot_nt(dyb, wd).astype(bf16).astype(f32)
            g_d[t] = dot_tn(hid_[l, :, gcols], dyb).astype(bf16).reshape(SIDE, FROWS, D)
            gt, up = gu_[l, :, gcols], gu_[l, :, ucols]
            s = jax.nn.sigmoid(gt)
            dgt = (dhid * up * s * (1.0 + gt * (1.0 - s))).astype(bf16)
            dup = (dhid * gt * s).astype(bf16)
            g_gu[:, :, gcols] = dot_tn(bn, dgt).astype(bf16).reshape(SIDE, BAND, FBAND)
            g_gu[:, :, ucols] = dot_tn(bn, dup).astype(bf16).reshape(SIDE, BAND, FBAND)
            acc2[...] += dot_nt(dgt, w_gu[l, :, :, gcols].reshape(D, FBAND))
            acc2[...] += dot_nt(dup, w_gu[l, :, :, ucols].reshape(D, FBAND))
            return c

        lax.fori_loop(0, SIDE, tile, 0)
        dbn = acc2[...]
        mid = mid_[l]
        r = factor_of(mid)
        _, gain = gains(l)
        gain_term[...] = (dbn * mid * r).astype(bf16)
        return dy + norm_back(mid, r, gain, dbn)

    def attention_back(l, dmid):
        dmb = dmid.astype(bf16)
        o = heads_in(o_.at[l])
        g_qo[:, :, OAT : OAT + 640] = jnp.concatenate(
            [dot_tn(o, dmb), jnp.zeros((D, 64), f32)], axis=1
        ).astype(bf16).reshape(SIDE, BAND, 640)
        dob = dot_nt(dmb, w_qo[l, :, :, OAT : OAT + D].reshape(D, D)).astype(bf16)
        for h in range(HEADS):
            do_h = dob[:, h * 64 : h * 64 + 64]
            dq_[h] = jnp.zeros((TOK, 64), f32)
            dob_[h] = do_h
        for g in range(KV_HEADS):
            do = dob_[3 * g : 3 * g + 3].reshape(GROUP, 64).astype(f32)
            og = o_[l, 3 * g : 3 * g + 3].reshape(GROUP, 64).astype(f32)
            delta_[g] = jnp.sum(do * og, axis=1, keepdims=True)

        def chunk(c, masked):
            kvb = kv[l, keys_at(c), :]
            dks, dvs = [], []
            for g in range(KV_HEADS):
                q = q8_[l, 3 * g : 3 * g + 3].reshape(GROUP, 64)
                do = dob_[3 * g : 3 * g + 3].reshape(GROUP, 64)
                k = kvb[:, g * 64 : g * 64 + 64]
                v = kvb[:, 192 + g * 64 : 256 + g * 64]
                s = dot_nt(q, k)
                if masked:
                    s = jnp.where(causal(), s, -1e30)
                p = jnp.exp(s - lse_[l, g])
                ds = (p * (dot_nt(do, v) - delta_[g])).astype(bf16)
                dq_[3 * g : 3 * g + 3] += dot(ds, k).reshape(3, TOK, 64)
                dks.append(dot_tn(ds, q))
                dvs.append(dot_tn(p.astype(bf16), do))
            dkv_s[keys_at(c), :] = jnp.concatenate(dks + dvs, axis=1).astype(bf16)

        def full(c, carry):
            chunk(c, False)
            for i in range(SIDE):
                dkv_start(l, c * SIDE + i)
            return carry

        lax.fori_loop(0, nfull, full, 0)
        chunk(nfull, True)

        def rest(j, carry):
            dkv_start(l, j)
            return carry

        lax.fori_loop(nfull * SIDE, sh, rest, 0)

    def finish_back(l, dmid_at):
        dkv_acc[...] = dkv_s[tokens, :].astype(f32)

        def add(d, c):
            arrived(dkv_r.at[l, d], at_dkv[l] + d)
            dkv_acc[...] += dkv_r[l, d].astype(f32)
            return c

        lax.fori_loop(1, SHARDS - sh, add, 0)
        dkv = dkv_acc[...]
        cos, sin = tables()
        dq = jnp.concatenate([dq_[h] for h in range(HEADS)], axis=1) * score_scale
        u = jnp.concatenate([dq, dkv[:, 0:192]], axis=1)
        back = u * cos - half_swap(u) * sin
        dqkv = jnp.concatenate([back, dkv[:, 192:384], jnp.zeros((TOK, 64), f32)], axis=1).astype(bf16)
        a = a_[l]
        gq = dot_tn(a, dqkv)
        da = dot_nt(dqkv, w_qo[l, :, :, 0:QKV].reshape(D, QKV))
        x = xs_[l]
        r = factor_of(x)
        gain, _ = gains(l)
        lane = lax.broadcasted_iota(jnp.int32, (TOK, 128), 1)
        e0 = jnp.where(lane == 64, 1.0, 0.0).astype(bf16)
        e1 = jnp.where(lane == 65, 1.0, 0.0).astype(bf16)
        cols = dot_tn((da * x * r).astype(bf16), e0) + dot_tn(gain_term[...], e1)
        g_qo[:, :, 0:896] = gq[:, 0:896].astype(bf16).reshape(SIDE, BAND, 896)
        g_qo[:, :, 896:1024] = (gq[:, 896:1024] + cols).astype(bf16).reshape(SIDE, BAND, 128)
        return dmid_at + norm_back(x, r, gain, da)

    kinds = (
        ("gu", 0, w_gu, g_gu, zr, ys, yr, xs, xr, fs, fr, GU),
        ("qo", 1, w_qo, g_qo, zr, ys, yr, xs, xr, fs, fr, QO),
        ("d", 1, w_d, g_d, zr_d, ys_d, yr_d, xs_d, xr_d, fs_d, fr_d, D),
    )
    at_rs = {k[0]: [take(1 + 3 + 3 + 3 + 1) for _ in range(2)] for k in kinds}

    def cut(ref, width):
        lead = (slice(None),) * (len(ref.shape) - 1)
        return ref.at[(*lead, pl.ds(0, width))]

    def of_core(kind):
        name, owner, w, g, zr, ys, yr, xs, xr, fs, fr, width = kind
        return owner, w, g, *[cut(r, width) for r in (zr, ys, yr, xs, xr, fs, fr)], width

    def free_weights(l):
        pl.semaphore_signal(credit.at[l], inc=1, device_id={"replica": sib}, device_id_type=MESH)

    def pair_start(l):
        pl.semaphore_wait(credit.at[l], 1)
        for kind in kinds:
            owner, w, g, *_ = of_core(kind)
            at = at_rs[kind[0]][l]

            @pl.when(core != owner)
            def _():
                copy(g, w.at[l], at, replica=sib).start()

    def tiles(width):
        step = 512 if width == GU else 128
        return step, width // step

    def rs_z_start(l):
        for kind in kinds:
            owner, w, g, zr, ys, yr, xs, xr, fs, fr, width = of_core(kind)
            at = at_rs[kind[0]][l]

            @pl.when(core == owner)
            def _():
                arrived(w.at[l], at)
                for d in (1, 2, 3, 0):
                    zt = lax.rem(z + d, SIDE)
                    if kind[0] == "d":
                        g[zt] = (g[zt].astype(f32) + w[l, zt].astype(f32)).astype(bf16)
                    else:
                        step, count = tiles(width)

                        def add(t, c):
                            cols = pl.ds(pl.multiple_of(t * step, 128), step)
                            g[zt, :, cols] = (
                                g[zt, :, cols].astype(f32) + w[l, zt, :, cols].astype(f32)
                            ).astype(bf16)
                            return c

                        lax.fori_loop(0, count, add, 0)
                    if d:
                        copy(g.at[zt], zr.at[d - 1], at + d, shard=z_peer(d)).start()

    def rs_y_start(l):
        for kind in kinds:
            owner, w, g, zr, ys, yr, xs, xr, fs, fr, width = of_core(kind)
            at = at_rs[kind[0]][l]

            @pl.when(core == owner)
            def _():
                for d in range(1, SIDE):
                    arrived(zr.at[d - 1], at + d)
                if kind[0] == "d":
                    tot = g[z].astype(f32)
                    for d in range(3):
                        tot += zr[d].astype(f32)
                    ys[...] = tot.astype(bf16)
                else:
                    step, count = tiles(width)

                    def add(t, c):
                        cols = pl.ds(pl.multiple_of(t * step, 128), step)
                        tot = g[z, :, cols].astype(f32)
                        for d in range(3):
                            tot += zr[d, :, cols].astype(f32)
                        for j in range(SIDE):
                            rows = tot[j * ROWS : j * ROWS + ROWS]
                            rows = jnp.concatenate([rows, jnp.zeros((PAD - ROWS, step), f32)], axis=0)
                            ys[j, :, cols] = rows.astype(bf16)
                        return c

                    lax.fori_loop(0, count, add, 0)
                for d in range(1, SIDE):
                    yt = lax.rem(y + d, SIDE)
                    copy(ys.at[yt], yr.at[d - 1], at + 3 + d, shard=y_peer(d)).start()

    def x_targets(l):
        for k in (1, 2, 3):
            other = 1 - sec if k >= 2 else sec
            where = {}
            if k >= 2:
                where["section"] = 1 - sec
            if k % 2:
                where["replica"] = far
            yield k, other == l, where

    def rs_x_start(l):
        for kind in kinds:
            owner, w, g, zr, ys, yr, xs, xr, fs, fr, width = of_core(kind)
            at = at_rs[kind[0]][l]

            @pl.when(core == owner)
            def _():
                for d in range(1, SIDE):
                    arrived(yr.at[d - 1], at + 3 + d)
                tot = ys[y].astype(f32)
                for d in range(3):
                    tot += yr[d].astype(f32)
                xs[...] = tot.astype(bf16)
                for k, hit, where in x_targets(l):
                    @pl.when(hit)
                    def _():
                        copy(xs, xr.at[k - 1], at + 6 + k, **where).start()

    def write_out(kind, tot):
        if kind[0] == "d":
            gd_ref[0] = tot
        elif kind[0] == "gu":
            gg_ref[0] = tot[0:ROWS, 0:FF]
            gu_ref[0] = tot[0:ROWS, FF:GU]
        else:
            gq_ref[0] = tot[0:ROWS, 0:576]
            gk_ref[0] = tot[0:ROWS, 576:768]
            gv_ref[0] = tot[0:ROWS, 768:960]
            go_ref[0] = tot[0:ROWS, OAT : OAT + D]
            gain_ref[...] = tot[0:ROWS, 896:1024]

    def rs_end_start(l):
        for kind in kinds:
            owner, w, g, zr, ys, yr, xs, xr, fs, fr, width = of_core(kind)
            at = at_rs[kind[0]][l]

            @pl.when((core == owner) & (sec == l))
            def _():
                for k in (1, 2, 3):
                    arrived(xr.at[k - 1], at + 6 + k)
                tot = xs[...].astype(f32)
                for k in range(3):
                    tot += xr[k].astype(f32)
                fs[...] = tot.astype(bf16)
                copy(fs, fr, at + 10, replica=sib).start()
                write_out(kind, tot)

    def rs_end(l):
        for kind in kinds:
            owner, w, g, zr, ys, yr, xs, xr, fs, fr, width = of_core(kind)
            at = at_rs[kind[0]][l]

            @pl.when((core != owner) & (sec == l))
            def _():
                arrived(fr, at + 10)
                write_out(kind, fr[...].astype(f32))

    def rs_sent(l):
        for kind in kinds:
            owner, w, g, zr, ys, yr, xs, xr, fs, fr, width = of_core(kind)
            at = at_rs[kind[0]][l]

            @pl.when(core != owner)
            def _():
                sent(g, at)

            @pl.when(core == owner)
            def _():
                for d in range(1, SIDE):
                    sent(zr.at[0], at + d)
                    sent(yr.at[0], at + 3 + d)
                for k, hit, where in x_targets(l):
                    @pl.when(hit)
                    def _():
                        sent(xs, at + 6 + k)

                @pl.when(sec == l)
                def _():
                    sent(fs, at + 10)

    def again():
        for d in range(1, SIDE):
            pl.semaphore_signal(credit.at[2], inc=1, device_id={"shard": y_peer(d)}, device_id_type=MESH)
            pl.semaphore_signal(credit.at[2], inc=1, device_id={"shard": z_peer(d)}, device_id_type=MESH)
        pl.semaphore_signal(credit.at[2], inc=1, device_id={"replica": sib}, device_id_type=MESH)
        pl.semaphore_signal(credit.at[2], inc=1, device_id={"replica": far}, device_id_type=MESH)
        pl.semaphore_signal(credit.at[2], inc=1, device_id={"section": 1 - sec}, device_id_type=MESH)
        pl.semaphore_signal(
            credit.at[2], inc=1, device_id={"section": 1 - sec, "replica": far}, device_id_type=MESH
        )

    def again_wait():
        pl.semaphore_wait(credit.at[2], 10)

    at_o = [take(1) for _ in range(2)]
    at_d = [take(1) for _ in range(2)]

    def hand_over(l, value, own_ref, send, recv, at):
        @pl.when(sec == l)
        def _():
            own_ref[0, sec, 0] = value

        @pl.when(sec != l)
        def _():
            send[...] = value
            copy(send, recv, at[l], section=1 - sec).start()

    def hand_over_end(own_ref, send, recv, at):
        for l in range(2):
            @pl.when(sec == l)
            def _():
                arrived(recv, at[l])
                own_ref[0, 1 - sec, 0] = recv[...]

            @pl.when(sec != l)
            def _():
                sent(send, at[l])

    x_start()
    for l in range(2):
        y_start(l)
        dz_start(l)
    for l in range(2):
        z_start(l)
        dy_start(l)
    for l in range(2):
        forward_on(l)
        d_forward_on(l)
    for l in range(2):
        gather_end(l)
        gather_sent(l)

    xs_[0] = x_ref[sec, 0].astype(f32)
    for l in range(2):
        project_in(l)
        kv_start(l)
        kv_wait(l)
        attend(l)
        out = after_attention(l).astype(bf16)
        hand_over(l, out, out_ref, osend, orecv, at_o)
        if l == 0:
            xs_[1] = out.astype(f32)
        kv_sent(l)

    dy = dy_ref[sec, 0].astype(f32)
    for l in (1, 0):
        dmid = ffn_back(l, dy)
        mid_[l] = dmid
        attention_back(l, dmid)
        dx = finish_back(l, mid_[l])
        hand_over(l, dx, dx_ref, dsend, drecv, at_d)
        dy = dx.astype(bf16).astype(f32)
        dkv_sent(l)
        free_weights(l)
        pair_start(l)
        if l == 0:
            again_wait()
        rs_z_start(l)
        rs_y_start(l)
        rs_x_start(l)
        rs_end_start(l)
        rs_end(l)
        rs_sent(l)
        if l == 1:
            again()
    hand_over_end(out_ref, osend, orecv, at_o)
    hand_over_end(dx_ref, dsend, drecv, at_d)
    assert used[0] <= SEMS, used[0]


SEMS = 320


def scratch():
    v = lambda *shape: pltpu.VMEM(shape, bf16)
    w = lambda *shape: pltpu.VMEM(shape, f32)
    return dict(
        stage=v(2, SIDE, PAD, GU), w_gu=v(2, SIDE, BAND, GU), w_qo=v(2, SIDE, BAND, QO),
        w_d=v(2, SIDE, SIDE, FROWS, D), kv=v(2, SHARDS * TOK, 384), dkv_s=v(SHARDS * TOK, 384),
        dkv_r=v(2, SHARDS, TOK, 384), scr=w(GROUP, SHARDS * TOK), mx=w(GROUP, 128), acc=w(GROUP, 128),
        xs_=w(2, TOK, D), a_=v(2, TOK, D), q8_=v(2, HEADS, TOK, 64), o_=v(2, HEADS, TOK, 64),
        lse_=w(2, KV_HEADS, GROUP, 1), mid_=w(2, TOK, D), bn_=v(2, TOK, D), gu_=w(2, TOK, GU),
        hid_=v(2, TOK, FF), dyb_=v(TOK, D), dob_=v(HEADS, TOK, 64), delta_=w(KV_HEADS, GROUP, 1),
        dq_=w(HEADS, TOK, 64), dkv_acc=w(TOK, 384), acc2=w(TOK, D), gain_term=v(TOK, D),
        g_gu=v(SIDE, BAND, GU), g_qo=v(SIDE, BAND, QO), g_d=v(SIDE, SIDE, FROWS, D),
        zr=v(3, BAND, GU), zr_d=v(3, SIDE, FROWS, D), ys=v(SIDE, PAD, GU), ys_d=v(SIDE, FROWS, D),
        yr=v(3, PAD, GU), yr_d=v(3, FROWS, D), xs=v(PAD, GU), xs_d=v(FROWS, D),
        xr=v(3, PAD, GU), xr_d=v(3, FROWS, D), fs=v(PAD, GU), fs_d=v(FROWS, D),
        fr=v(PAD, GU), fr_d=v(FROWS, D),
        osend=v(TOK, D), orecv=v(TOK, D), dsend=w(TOK, D), drecv=w(TOK, D),
        ssem=pltpu.SemaphoreType.DMA((SEMS,)), rsem=pltpu.SemaphoreType.DMA((SEMS,)),
        credit=pltpu.SemaphoreType.REGULAR((3,)),
    )


def kernel(*refs):
    body(*refs)


def local(
    inputs, out_grad, w_query, w_key, w_value, w_out, w_gate, w_up, w_down, gain_attn, gain_ffn
):
    shard_index = lax.axis_index("shard")
    positions = shard_index * TOK + jnp.arange(TOK, dtype=jnp.int32)
    half = HEAD_DIM // 2
    inverse = rope_base ** (-(jnp.arange(half, dtype=f32) * 2.0 / HEAD_DIM))
    angles = positions.astype(f32)[:, None] * inverse[None, :]
    cos, sin = jnp.cos(angles), jnp.sin(angles)
    cos = jnp.concatenate([cos] * 4, axis=1)
    sin = jnp.concatenate([-sin, sin, -sin, sin], axis=1)
    more = ((0, PAD - ROWS), (0, 0))
    p0 = jnp.pad(jnp.concatenate([w_gate[0], w_up[0]], axis=1), more)
    gain_cols = jnp.stack([gain_attn[0], gain_ffn[0]], axis=1)
    p1 = jnp.concatenate(
        [w_query[0], w_key[0], w_value[0], gain_cols, jnp.zeros((ROWS, 62), bf16), w_out[0],
         jnp.zeros((ROWS, 64), bf16)], axis=1,
    )
    p1 = jnp.pad(p1, more)
    whole = pl.BlockSpec(memory_space=pltpu.VMEM)
    shapes = (
        ((1, 2, 1, TOK, D), bf16), ((1, 2, 1, TOK, D), f32),
        ((1, ROWS, 576), f32), ((1, ROWS, 192), f32), ((1, ROWS, 192), f32), ((1, ROWS, 576), f32),
        ((1, ROWS, FF), f32), ((1, ROWS, FF), f32), ((1, FROWS, D), f32), ((ROWS, 128), f32),
    )
    res = pl.pallas_call(
        kernel,
        out_shape=[jax.ShapeDtypeStruct(s, t) for s, t in shapes],
        in_specs=[whole] * 7,
        out_specs=[whole] * len(shapes),
        scratch_shapes=list(scratch().values()),
        compiler_params=pltpu.CompilerParams(
            collective_id=0, has_side_effects=True, vmem_limit_bytes=63 * 1024 * 1024
        ),
        name="two_layers",
    )(inputs, out_grad, p0, p1, w_down[0], cos, sin)
    out, dx, gq, gk, gv, go, gg, gu, gd, gain = res
    return (out, dx, gq, gk, gv, go, gg, gu, gd, gain[:, 64][None], gain[:, 65][None])


def solution(mesh):
    return jax.shard_map(
        local,
        mesh=mesh,
        in_specs=(
            P(None, "replica", "shard", None),
            P(None, "replica", "shard", None),
            P("section", "shard", None),
            P("section", "shard", None),
            P("section", "shard", None),
            P("section", "shard", None),
            P("section", "shard", None),
            P("section", "shard", None),
            P("section", "shard", None),
            P("section", "shard"),
            P("section", "shard"),
        ),
        out_specs=(
            P("section", None, "replica", "shard", None),
            P("section", None, "replica", "shard", None),
            P("section", "shard", None),
            P("section", "shard", None),
            P("section", "shard", None),
            P("section", "shard", None),
            P("section", "shard", None),
            P("section", "shard", None),
            P("section", "shard", None),
            P("section", "shard"),
            P("section", "shard"),
        ),
        check_vma=False,
    )
```

time: 1270 us -> 358 us (0.28)
  waiting for transfers between devices: 542 us -> 0 us
  Pallas kernels: 0 us -> 341 us
  blocking collectives: 327 us -> 0 us
  matrix products: 150 us -> 0 us
  local copies, waits for them, and re-layouts: 126 us -> 14.3 us
  other arithmetic: 64 us -> 1.88 us
  starting transfers between devices: 34.3 us -> 0 us
  between operations: 18.9 us -> 0.77 us
    unnamed x29 -> x0, waiting for transfers between devices: 459 us -> none
    pallas_call x0 -> x1, Pallas kernels: none -> 341 us  [local(): pl.pallas_call(kernel, out_shape=[jax.ShapeDtypeStruct(s, t) for s, t in...]
    all_gather x10 -> x0, blocking collectives: 204 us -> none  [the longest x3 60 us: layer_forward(): lax.all_gather(keys_local, 'shard', axis=1, tiled=True)]
    dot_general x81 -> x0, matrix products: 150 us -> none  [the longest x21 45 us: outer_sum(): jnp.einsum('scd,sce->de', left, right, preferred_element_type=jnp.float32)]
    unnamed x3 -> x0, blocking collectives: 123 us -> none
    unnamed x397 -> x41, local copies, waits for them, and re-layouts: 121 us -> 10.4 us
    psum x2 -> x0, waiting for transfers between devices: 79 us -> none  [the longest x1 42.8 us: local(): lax.psum(summed[0].astype(jnp.bfloat16), 'replica').astype(jnp.float32)]
    convert_element_type x27 -> x1, other arithmetic: 46.1 us -> 0.01 us  [local(): angles = positions.astype(f32)[:, None] * inverse[None, :]]
  transfers between devices with their start and end apart: 25 -> 0, of which waited for: 12 -> 0; matrix products, arithmetic and copies ran while one was open for 19% -> 0% of each run, Pallas kernels for 0% -> 0%
where the time goes in v1:
time: 358 us
  Pallas kernels  341 us (95%)
  local copies, waits for them, and re-layouts  14.3 us (4%)
    pallas_call x1, Pallas kernels, local(): pl.pallas_call(kernel, out_shape=[jax.ShapeDtypeStruct(s, t) for s, t in...  341 us
    unnamed x41, local copies, waits for them, and re-layouts  10.4 us

profile of v1, /device:TPU:1, one launch (start us, length us, event | category | flops | bytes accessed | tf_op | source)
XLA Modules:
  0.0 357.8 jit_solution(12658214989145499100)
XLA Ops:
  0.6 0.0 copy-start.11
  0.7 0.0 copy-start.14
  0.7 0.8 copy.46
  1.5 0.8 copy.47
  2.2 0.0 copy-done.11
  2.3 0.0 copy-done.14
  2.3 0.9 concatenate.13
  3.2 0.7 pad.9.refs_3_
  3.9 0.3 fusion.3
  4.2 0.0 copy-start.6
  4.2 0.0 copy-start.7
  4.2 0.8 pad_maximum_fusion
  5.0 0.0 copy-start.1
  5.0 0.1 copy-done.6
  5.1 0.1 copy-done.7
  5.2 0.7 fusion.2.refs_2_
  5.9 0.1 copy-done.1
  6.0 0.0 copy-start.2
  6.0 0.9 copy.49.refs_0_
  6.9 0.1 copy-done.2
  7.0 0.9 copy.50.refs_1_
  7.9 340.9 %two_layers.1 = (bf16[1,2,1,128,576]{4,3,2,1,0:T(8,128)(2,1)}, f32[1,2,1,128,576]{4,3,2,1,0:T(8,128)}, f32[1,36,576]{2,1,0:T(8,128)}, f32[1,36,192]{2,1,0:T(8,12...) custom-call(bf16[2,1,128,576]{3,2,1,0:T(8,128)(2,1)} %copy.49.refs_0, ...), custom_call_target="tpu_custom_call" | custom-call | tf_op jit(solution)/shard_map/two_layers/pallas_call | solution.py:829
  348.8 0.0 copy-start.10
  348.8 0.0 copy-start.13
  348.8 0.0 copy-start.9
  348.8 1.9 copy.51
  350.7 0.0 copy-done.10
  350.7 0.0 copy-start.12
  350.7 0.7 slice_reduce_fusion
  351.4 0.0 copy-done.13
  351.4 0.0 copy-start.8
  351.4 0.0 copy-start.4
  351.4 0.7 copy.54
  352.1 0.0 copy-done.12
  352.1 0.0 copy-start.3
  352.1 0.7 copy.55
  352.7 0.0 copy-done.9
  352.7 0.7 copy.53
  353.5 0.0 copy-done.8
  353.5 0.7 copy.56
  354.2 0.0 copy-done.4
  354.2 0.9 copy.57
  355.1 0.0 copy-done.3
  355.1 0.9 copy.58
  356.0 0.0 copy-done
  356.0 1.0 copy.52
  357.1 0.0 copy-done.5
  357.1 0.7 copy.60
  (6 shorter events, 0.0 us)
Async XLA Ops:
  0.6 1.6 copy-start.11
  0.7 1.6 copy-start.14
  4.2 0.9 copy-start.6
  4.2 1.0 copy-start.7
  5.0 1.0 copy-start.1
  6.0 1.0 copy-start.2
  348.8 1.9 copy-start.10
  348.8 2.6 copy-start.13
  348.8 3.9 %copy-start.9 = (f32[1,36,576]{2,1,0:T(8,128)S(1)}, f32[1,36,576]{2,1,0:T(8,128)}, u32[]{:S(2)}) copy-start(f32[1,36,576]{2,1,0:T(8,128)} %get-tuple-element.55) | copy-start | bytes 248836
  350.7 1.4 copy-start.12
  351.4 2.1 copy-start.8
  351.4 2.8 copy-start.4
  352.1 3.1 copy-start.3
  352.7 3.3 copy-start
  356.0 1.1 copy-start.5

commit v2 on v1

v2 whole, which is shorter than its diff:
```python
import functools

import jax
import jax.numpy as jnp
from jax import lax
from jax.experimental import pallas as pl
from jax.experimental.pallas import tpu as pltpu
from jax.sharding import PartitionSpec as P

HEADS = 9
KV_HEADS = 3
HEAD_DIM = 64
D = 576
FF = 1536
TOK = 128
SHARDS = 16
SIDE = 4
ROWS = 36
PAD = 48
BAND = SIDE * ROWS
FROWS = 96
FBAND = SIDE * FROWS
GU = 2 * FF
QKV = 1024
OUT = 640
CHUNK = 512
GROUP = 3 * TOK

bf16 = jnp.bfloat16
f32 = jnp.float32
MESH = pl.DeviceIdType.MESH
epsilon = 1e-05
rope_base = 100000.0
score_scale = 0.125


def dot(a, b):
    return lax.dot_general(a, b, (((1,), (0,)), ((), ())), preferred_element_type=f32)


def dot_nt(a, b):
    return lax.dot_general(a, b, (((1,), (1,)), ((), ())), preferred_element_type=f32)


def dot_tn(a, b):
    return lax.dot_general(a, b, (((0,), (0,)), ((), ())), preferred_element_type=f32)


def factor_of(v):
    return lax.rsqrt(jnp.mean(v * v, axis=-1, keepdims=True) + epsilon)


def norm_back(v, r, gain, up):
    scaled = gain * up
    return r * scaled - v * (r * r * r) * jnp.mean(scaled * v, axis=-1, keepdims=True)


def half_swap(u):
    width = u.shape[1]
    lane = lax.broadcasted_iota(jnp.int32, u.shape, 1)
    first = lax.rem(lane, HEAD_DIM) < HEAD_DIM // 2
    return jnp.where(first, pltpu.roll(u, width - 32, 1), pltpu.roll(u, 32, 1))


def body(
    x_ref, dy_ref, p0_ref, pq_ref, po_ref, pd_ref, cos_ref, sin_ref,
    out_ref, dx_ref, gq_ref, gk_ref, gv_ref, go_ref, gg_ref, gu_ref, gd_ref, gain_ref,
    stage_gu, stage_q, stage_o, w_gu, w_q, w_o, w_d, kv, dkv_r, scr, mx, acc,
    xs_, a_, q8_, o_, lse_, mid_, bn_, gu_,
    dyb_, dob_, delta_, dq_, dkv_acc, acc2, gain_term,
    g_gu, g_q, g_o, g_d, xg,
    zr_gu, zr_q, zr_o, zr_d, ys_gu, ys_q, ys_o, ys_d, yr_gu, yr_q, yr_o, yr_d,
    xs_gu, xs_q, xs_o, xs_d, xr_gu, xr_q, xr_o, xr_d, fs_gu, fs_q, fs_o, fs_d, fr_gu, fr_q, fr_o, fr_d,
    osend, orecv, dsend, drecv,
    ssem, rsem, credit,
):
    sec = lax.axis_index("section")
    sh = lax.axis_index("shard")
    rep = lax.axis_index("replica")
    z, y = lax.div(sh, SIDE), lax.rem(sh, SIDE)
    core = lax.rem(rep, 2)
    sib = rep + 1 - 2 * core
    far = lax.rem(rep + 2, 4)
    used = [0]

    def take(n):
        at = used[0]
        used[0] += n
        return at

    def copy(src, dst, at, **dev):
        return pltpu.make_async_remote_copy(
            src_ref=src, dst_ref=dst, send_sem=ssem.at[at], recv_sem=rsem.at[at],
            device_id=dev, device_id_type=MESH,
        )

    def arrived(dst, at):
        copy(dst, dst, at, shard=sh).wait_recv()

    def sent(src, at):
        copy(src, src, at, shard=sh).wait_send()

    def y_peer(d):
        return z * SIDE + lax.rem(y + d, SIDE)

    def z_peer(d):
        return lax.rem(z + d, SIDE) * SIDE + y

    def z_from(d):
        return lax.rem(z + SIDE - d, SIDE)

    def y_from(d):
        return lax.rem(y + SIDE - d, SIDE)

    last = pl.ds(pl.multiple_of(lax.div(sh, SIDE) * CHUNK, CHUNK), CHUNK)
    for l in range(2):
        kv[l, last, :] = jnp.zeros((CHUNK, 384), bf16)
    barrier = pltpu.get_barrier_semaphore()

    def greet(d, c):
        pl.semaphore_signal(barrier, inc=1, device_id={"shard": lax.rem(sh + d, SHARDS)}, device_id_type=MESH)
        return c

    lax.fori_loop(1, SHARDS, greet, 0)
    pl.semaphore_signal(barrier, inc=1, device_id={"replica": sib}, device_id_type=MESH)
    pl.semaphore_signal(barrier, inc=1, device_id={"replica": far}, device_id_type=MESH)
    pl.semaphore_signal(barrier, inc=1, device_id={"section": 1 - sec}, device_id_type=MESH)
    pl.semaphore_signal(barrier, inc=1, device_id={"section": 1 - sec, "replica": far}, device_id_type=MESH)
    pl.semaphore_wait(barrier, SHARDS - 1 + 4)

    mine = pl.ds(pl.multiple_of(sec * FF, 128), FF)
    theirs = pl.ds(pl.multiple_of((1 - sec) * FF, 128), FF)

    class Gather:
        def __init__(self, owner, send, keep, stage, w, cols, width):
            self.owner, self.send, self.keep, self.stage, self.w, self.width = owner, send, keep, stage, w, width
            self.cols = cols
            self.at_x = take(1)
            self.at_y = [take(3) for _ in range(2)]
            self.at_z = [take(3) for _ in range(2)]
            self.at_f = [take(4) for _ in range(2)]

        def band(self, l, j):
            return self.w.at[l, j, :, self.cols]

    kgu = Gather(0, p0_ref.at[:, theirs], p0_ref.at[:, mine], stage_gu, w_gu, mine, FF)
    kq = Gather(1, pq_ref, pq_ref, stage_q, w_q, pl.ds(0, QKV), QKV)
    ko = Gather(1, po_ref, po_ref, stage_o, w_o, pl.ds(0, OUT), OUT)
    at_xd = take(1)
    at_dz = [take(3) for _ in range(2)]
    at_dy = [take(3) for _ in range(2)]
    at_df = [take(1) for _ in range(2)]
    at_swap = [take(4) for _ in range(2)]
    at_sf = [take(4) for _ in range(2)]

    def x_start(k):
        @pl.when(core == k.owner)
        def _():
            copy(k.send, k.stage.at[sec, y], k.at_x, section=1 - sec).start()
            k.stage[sec, y] = k.keep[...]

    def dx_start():
        @pl.when(core == 1)
        def _():
            copy(pd_ref, w_d.at[sec, z, y], at_xd, section=1 - sec).start()
            w_d[sec, z, y] = pd_ref[...]

    def y_start(k, l):
        @pl.when(core == k.owner)
        def _():
            own = k.stage.at[l, y]

            @pl.when(sec != l)
            def _():
                arrived(own, k.at_x)

            for d in (2, 1, 3):
                copy(own, own, k.at_y[l] + d - 1, shard=y_peer(d)).start()

    def dz_start(l):
        @pl.when(core == 1)
        def _():
            own = w_d.at[l, z, y]

            @pl.when(sec != l)
            def _():
                arrived(own, at_xd)

            for d in (2, 1, 3):
                copy(own, own, at_dz[l] + d - 1, shard=z_peer(d)).start()

    def z_start(k, l):
        @pl.when(core == k.owner)
        def _():
            for d in range(1, SIDE):
                arrived(k.stage.at[l, y_from(d)], k.at_y[l] + d - 1)
            own = k.band(l, z)
            for at in range(0, k.width, 128):
                parts = [k.stage[l, j, :, at : at + 128][0:ROWS].astype(f32) for j in range(SIDE)]
                own[:, at : at + 128] = jnp.concatenate(parts, axis=0).astype(bf16)
            for d in (2, 1, 3):
                copy(own, own, k.at_z[l] + d - 1, shard=z_peer(d)).start()
            copy(own, own, k.at_f[l], replica=sib).start()

    def dy_start(l):
        @pl.when(core == 1)
        def _():
            for d in range(1, SIDE):
                arrived(w_d.at[l, z_from(d), y], at_dz[l] + d - 1)
            own = w_d.at[l, :, y]
            for d in (2, 1, 3):
                copy(own, own, at_dy[l] + d - 1, shard=y_peer(d)).start()

    def z_end(k, l):
        @pl.when(core == k.owner)
        def _():
            for d in (1, 3, 2):
                got = k.band(l, z_from(d))
                arrived(got, k.at_z[l] + d - 1)
                copy(got, got, k.at_f[l] + d, replica=sib).start()
            if k is kgu:
                for j in range(SIDE):
                    got = k.band(l, j)
                    copy(got, got, at_swap[l] + j, **swap_to(j)).start()

    def swap_to(j):
        return {"section": 1 - sec} if j < 2 else {"section": 1 - sec, "replica": far}

    def swap_end(l):
        @pl.when(core == 0)
        def _():
            for j in range(SIDE):
                got = w_gu.at[l, j, :, theirs]
                arrived(got, at_swap[l] + j)
                copy(got, got, at_sf[l] + j, replica=sib).start()

    def d_forward_on(l):
        @pl.when(core == 1)
        def _():
            for d in range(1, SIDE):
                arrived(w_d.at[l, :, y_from(d)], at_dy[l] + d - 1)
            copy(w_d.at[l], w_d.at[l], at_df[l], replica=sib).start()

    def gather_end(k, l):
        @pl.when(core != k.owner)
        def _():
            arrived(k.band(l, z), k.at_f[l])
            for d in range(1, SIDE):
                arrived(k.band(l, z_from(d)), k.at_f[l] + d)
            if k is kgu:
                for j in range(SIDE):
                    arrived(w_gu.at[l, j, :, theirs], at_sf[l] + j)

    def d_gather_end(l):
        @pl.when(core == 0)
        def _():
            arrived(w_d.at[l], at_df[l])

    def gather_sent():
        for l in range(2):
            for k in (kgu, kq, ko):
                @pl.when(core == k.owner)
                def _():
                    @pl.when(sec == l)
                    def _():
                        sent(k.send, k.at_x)

                    for d in range(1, SIDE):
                        sent(k.stage.at[l, y], k.at_y[l] + d - 1)
                        sent(k.band(l, z), k.at_z[l] + d - 1)
                        sent(k.band(l, z), k.at_f[l] + d)
                    sent(k.band(l, z), k.at_f[l])
                    if k is kgu:
                        for j in range(SIDE):
                            sent(k.band(l, j), at_swap[l] + j)
                            sent(k.band(l, j), at_sf[l] + j)

            @pl.when(core == 1)
            def _():
                @pl.when(sec == l)
                def _():
                    sent(pd_ref, at_xd)

                for d in range(1, SIDE):
                    sent(w_d.at[l, z, y], at_dz[l] + d - 1)
                    sent(w_d.at[l, :, y], at_dy[l] + d - 1)
                sent(w_d.at[l], at_df[l])

    at_kv = [take(SHARDS) for _ in range(2)]
    at_dkv = [take(SHARDS) for _ in range(2)]
    tokens = pl.ds(pl.multiple_of(sh * TOK, TOK), TOK)

    def kv_start(l):
        own = kv.at[l, tokens]

        def go(d, c):
            copy(own, own, at_kv[l] + d, shard=sh + d).start()
            return c

        lax.fori_loop(1, SHARDS - sh, go, 0)

    def kv_wait(l):
        def go(d, c):
            arrived(kv.at[l, pl.ds(pl.multiple_of((sh - d) * TOK, TOK), TOK)], at_kv[l] + d)
            return c

        lax.fori_loop(1, sh + 1, go, 0)

    def kv_sent(l):
        def go(d, c):
            sent(kv.at[l, tokens], at_kv[l] + d)
            return c

        lax.fori_loop(1, SHARDS - sh, go, 0)

    def dkv_start(l, j):
        src = kv.at[l, pl.ds(pl.multiple_of(j * TOK, TOK), TOK)]
        copy(src, dkv_r.at[l, sh - j - 1], at_dkv[l] + sh - j, shard=j).start()

    def dkv_sent(l):
        def go(d, c):
            sent(kv.at[l, pl.ds(0, TOK)], at_dkv[l] + d)
            return c

        lax.fori_loop(1, sh + 1, go, 0)

    def gains(l):
        tile = w_q[l, :, :, 896:1024].reshape(D, 128)
        row = lax.broadcasted_iota(jnp.int32, (8, 128), 0)
        lane = lax.broadcasted_iota(jnp.int32, (8, 128), 1)
        pick = jnp.where(lane == row + 64, 1.0, 0.0).astype(bf16)
        both = dot_nt(pick, tile)
        return both[0:1], both[1:2]

    nfull = lax.div(sh, SIDE)

    def causal():
        row = lax.broadcasted_iota(jnp.int32, (GROUP, CHUNK), 0)
        col = lax.broadcasted_iota(jnp.int32, (GROUP, CHUNK), 1)
        return col <= lax.rem(sh, SIDE) * TOK + lax.rem(row, TOK)

    def keys_at(c):
        return pl.ds(pl.multiple_of(c * CHUNK, CHUNK), CHUNK)

    def tables():
        cos = jnp.concatenate([cos_ref[...]] * 6, axis=1)
        sin = jnp.concatenate([sin_ref[...]] * 6, axis=1)
        return cos, sin

    def project_in(l):
        x = xs_[l]
        gain, _ = gains(l)
        a = (x * factor_of(x) * gain).astype(bf16)
        a_[l] = a
        qkv = dot(a, w_q[l].reshape(D, QKV))
        cos, sin = tables()
        u = qkv[:, 0:768]
        turned = u * cos + half_swap(u) * sin
        for h in range(HEADS):
            head = turned[:, h * 64 : h * 64 + 64].astype(bf16)
            q8_[l, h] = (head.astype(f32) * score_scale).astype(bf16)
        block = jnp.concatenate([turned[:, 576:768], qkv[:, 768:960]], axis=1).astype(bf16)
        kv[l, tokens] = block

    def attend(l, g):
        if True:
            q = q8_[l, 3 * g : 3 * g + 3].reshape(GROUP, 64)

            def keep(c, s):
                scr[:, keys_at(c)] = s
                top = jnp.maximum(
                    jnp.maximum(s[:, 0:128], s[:, 128:256]), jnp.maximum(s[:, 256:384], s[:, 384:512])
                )
                mx[...] = jnp.maximum(mx[...], top)

            def scores(c):
                k = kv[l, keys_at(c), :][:, g * 64 : g * 64 + 64]
                return dot_nt(q, k)

            mx[...] = jnp.full_like(mx, -1e30)

            def first(c, carry):
                keep(c, scores(c))
                return carry

            lax.fori_loop(0, nfull, first, 0)
            keep(nfull, jnp.where(causal(), scores(nfull), -1e30))
            peak = jnp.max(mx[...], axis=1, keepdims=True)
            acc[...] = jnp.zeros_like(acc)

            def second(c, carry):
                p = jnp.exp(scr[:, keys_at(c)] - peak).astype(bf16)
                v = kv[l, keys_at(c), :][:, 192 + g * 64 : 256 + g * 64]
                v = jnp.concatenate([v, jnp.ones_like(v)], axis=1)
                acc[...] += dot(p, v)
                return carry

            lax.fori_loop(0, nfull + 1, second, 0)
            total = acc[:, 64:65]
            mixed = (acc[:, 0:64] / total).astype(bf16)
            lse_[l, g] = peak + jnp.log(total)
            o_[l, 3 * g : 3 * g + 3] = mixed.reshape(3, TOK, 64)

    def heads_in(ref):
        return jnp.concatenate([ref[h] for h in range(HEADS)], axis=1)

    def after_attention(l):
        o = heads_in(o_.at[l])
        mid = xs_[l] + dot(o, w_o[l, :, :, 0:D].reshape(D, D))
        mid_[l] = mid
        _, gain = gains(l)
        bn_[l] = (mid * factor_of(mid) * gain).astype(bf16)
        acc2[...] = mid

        def tile(t, c):
            gcols = pl.ds(pl.multiple_of(t * FBAND, 128), FBAND)
            ucols = pl.ds(pl.multiple_of(FF + t * FBAND, 128), FBAND)
            bn = bn_[l]
            gt = dot(bn, w_gu[l, :, :, gcols].reshape(D, FBAND))
            up = dot(bn, w_gu[l, :, :, ucols].reshape(D, FBAND))
            gu_[l, :, gcols] = gt
            gu_[l, :, ucols] = up
            hid = (gt * jax.nn.sigmoid(gt) * up).astype(bf16)
            acc2[...] += dot(hid, w_d[l, t].reshape(FBAND, D))
            return c

        lax.fori_loop(0, SIDE, tile, 0)
        return acc2[...]

    def ffn_back(l, dy):
        dyb_[...] = dy.astype(bf16)
        acc2[...] = jnp.zeros_like(acc2)

        def tile(t, c):
            gcols = pl.ds(pl.multiple_of(t * FBAND, 128), FBAND)
            ucols = pl.ds(pl.multiple_of(FF + t * FBAND, 128), FBAND)
            dyb = dyb_[...]
            bn = bn_[l]
            wd = w_d[l, t].reshape(FBAND, D)
            dhid = dot_nt(dyb, wd).astype(bf16).astype(f32)
            gt, up = gu_[l, :, gcols], gu_[l, :, ucols]
            s = jax.nn.sigmoid(gt)
            hid = (gt * s * up).astype(bf16)
            g_d[t] = dot_tn(hid, dyb).astype(bf16).reshape(SIDE, FROWS, D)
            dgt = (dhid * up * s * (1.0 + gt * (1.0 - s))).astype(bf16)
            dup = (dhid * gt * s).astype(bf16)
            g_gu[:, :, gcols] = dot_tn(bn, dgt).astype(bf16).reshape(SIDE, BAND, FBAND)
            g_gu[:, :, ucols] = dot_tn(bn, dup).astype(bf16).reshape(SIDE, BAND, FBAND)
            acc2[...] += dot_nt(dgt, w_gu[l, :, :, gcols].reshape(D, FBAND))
            acc2[...] += dot_nt(dup, w_gu[l, :, :, ucols].reshape(D, FBAND))
            return c

        lax.fori_loop(0, SIDE, tile, 0)
        dbn = acc2[...]
        mid = mid_[l]
        r = factor_of(mid)
        _, gain = gains(l)
        gain_term[...] = (dbn * mid * r).astype(bf16)
        return dy + norm_back(mid, r, gain, dbn)

    def out_back(l, dmid):
        dmb = dmid.astype(bf16)
        o = heads_in(o_.at[l])
        g_o[...] = jnp.concatenate(
            [dot_tn(o, dmb), jnp.zeros((D, 64), f32)], axis=1
        ).astype(bf16).reshape(SIDE, BAND, 640)
        dob = dot_nt(dmb, w_o[l, :, :, 0:D].reshape(D, D)).astype(bf16)
        for h in range(HEADS):
            do_h = dob[:, h * 64 : h * 64 + 64]
            dq_[h] = jnp.zeros((TOK, 64), f32)
            dob_[h] = do_h

    def attention_back(l):
        for g in range(KV_HEADS):
            do = dob_[3 * g : 3 * g + 3].reshape(GROUP, 64).astype(f32)
            og = o_[l, 3 * g : 3 * g + 3].reshape(GROUP, 64).astype(f32)
            delta_[g] = jnp.sum(do * og, axis=1, keepdims=True)

        def chunk(c, masked):
            kvb = kv[l, keys_at(c), :]
            dks, dvs = [], []
            for g in range(KV_HEADS):
                q = q8_[l, 3 * g : 3 * g + 3].reshape(GROUP, 64)
                do = dob_[3 * g : 3 * g + 3].reshape(GROUP, 64)
                k = kvb[:, g * 64 : g * 64 + 64]
                v = kvb[:, 192 + g * 64 : 256 + g * 64]
                s = dot_nt(q, k)
                if masked:
                    s = jnp.where(causal(), s, -1e30)
                p = jnp.exp(s - lse_[l, g])
                ds = (p * (dot_nt(do, v) - delta_[g])).astype(bf16)
                dq_[3 * g : 3 * g + 3] += dot(ds, k).reshape(3, TOK, 64)
                dks.append(dot_tn(ds, q))
                dvs.append(dot_tn(p.astype(bf16), do))
            kv[l, keys_at(c), :] = jnp.concatenate(dks + dvs, axis=1).astype(bf16)

        def full(c, carry):
            chunk(c, False)
            for i in range(SIDE):
                dkv_start(l, c * SIDE + i)
            return carry

        lax.fori_loop(0, nfull, full, 0)
        chunk(nfull, True)

        def rest(j, carry):
            dkv_start(l, j)
            return carry

        lax.fori_loop(nfull * SIDE, sh, rest, 0)

    def finish_back(l, dmid_at):
        dkv_acc[...] = kv[l, tokens, :].astype(f32)

        def add(d, c):
            arrived(dkv_r.at[l, d - 1], at_dkv[l] + d)
            dkv_acc[...] += dkv_r[l, d - 1].astype(f32)
            return c

        lax.fori_loop(1, SHARDS - sh, add, 0)
        dkv = dkv_acc[...]
        cos, sin = tables()
        dq = jnp.concatenate([dq_[h] for h in range(HEADS)], axis=1) * score_scale
        u = jnp.concatenate([dq, dkv[:, 0:192]], axis=1)
        back = u * cos - half_swap(u) * sin
        dqkv = jnp.concatenate([back, dkv[:, 192:384], jnp.zeros((TOK, 64), f32)], axis=1).astype(bf16)
        a = a_[l]
        gq = dot_tn(a, dqkv)
        da = dot_nt(dqkv, w_q[l].reshape(D, QKV))
        x = xs_[l]
        r = factor_of(x)
        gain, _ = gains(l)
        lane = lax.broadcasted_iota(jnp.int32, (TOK, 128), 1)
        e0 = jnp.where(lane == 64, 1.0, 0.0).astype(bf16)
        e1 = jnp.where(lane == 65, 1.0, 0.0).astype(bf16)
        cols = dot_tn((da * x * r).astype(bf16), e0) + dot_tn(gain_term[...], e1)
        g_q[:, :, 0:896] = gq[:, 0:896].astype(bf16).reshape(SIDE, BAND, 896)
        g_q[:, :, 896:1024] = (gq[:, 896:1024] + cols).astype(bf16).reshape(SIDE, BAND, 128)
        return dmid_at + norm_back(x, r, gain, da)

    class Sum:
        def __init__(self, name, owner, w, cols, g, zr, ys, yr, xs, xr, fs, fr, width):
            self.name, self.owner, self.w, self.cols, self.g = name, owner, w, cols, g
            self.zr, self.ys, self.yr, self.xs, self.xr, self.fs, self.fr = zr, ys, yr, xs, xr, fs, fr
            self.width = width
            self.at = [take(12) for _ in range(2)]
            self.free = credits(2)
            self.again_z, self.again_y = credits(1), credits(1)

        def band(self, l, j):
            return self.w.at[l, j] if self.name == "d" else self.w.at[l, j, :, self.cols]

    granted = [0]

    def credits(n):
        at = granted[0]
        granted[0] += n
        return at

    sgu = Sum("gu", 0, w_gu, mine, g_gu, zr_gu, ys_gu, yr_gu, xs_gu, xr_gu, fs_gu, fr_gu, FF)
    sq = Sum("q", 1, w_q, pl.ds(0, QKV), g_q, zr_q, ys_q, yr_q, xs_q, xr_q, fs_q, fr_q, QKV)
    so = Sum("o", 1, w_o, pl.ds(0, OUT), g_o, zr_o, ys_o, yr_o, xs_o, xr_o, fs_o, fr_o, OUT)
    sd = Sum("d", 1, w_d, None, g_d, zr_d, ys_d, yr_d, xs_d, xr_d, fs_d, fr_d, D)
    at_rswap = [take(4) for _ in range(2)]
    swap_again = credits(1)

    def pair_start(k, l):
        pl.semaphore_signal(credit.at[k.free + l], inc=1, device_id={"replica": sib}, device_id_type=MESH)
        pl.semaphore_wait(credit.at[k.free + l], 1)

        @pl.when(core != k.owner)
        def _():
            copy(k.g, k.w.at[l], k.at[l], replica=sib).start()

    def pair_sent(k, l):
        @pl.when(core != k.owner)
        def _():
            sent(k.g, k.at[l])

    def add_into(dst, src, width):
        step = 256 if width % 256 == 0 else 128

        def add(t, c):
            cols = pl.ds(pl.multiple_of(t * step, 128), step)
            dst[:, cols] = (dst[:, cols].astype(f32) + src[:, cols].astype(f32)).astype(bf16)
            return c

        lax.fori_loop(0, width // step, add, 0)

    def rs_swap_start(l):
        @pl.when(core == 0)
        def _():
            arrived(w_gu.at[l], sgu.at[l])
            if l == 0:
                pl.semaphore_wait(credit.at[swap_again], 2)
            for j in (0, 2, 1, 3):
                src = w_gu.at[l, j, :, theirs]
                add_into(src, g_gu.at[j, :, theirs], FF)
                copy(src, xg.at[j], at_rswap[l] + j, **swap_to(j)).start()
            for j in range(SIDE):
                add_into(w_gu.at[l, j, :, mine], g_gu.at[j, :, mine], FF)

    def rs_z_start(k, l):
        @pl.when(core == k.owner)
        def _():
            if k is not sgu:
                arrived(k.w.at[l], k.at[l])
            if l == 0:
                pl.semaphore_wait(credit.at[k.again_z], 3)
            for d in (2, 1, 3, 0):
                zt = lax.rem(z + d, SIDE)
                part = k.band(l, zt)
                if k is sd:
                    part[...] = (part[...].astype(f32) + k.g[zt].astype(f32)).astype(bf16)
                elif k is sgu:
                    arrived(xg.at[zt], at_rswap[l] + zt)
                    add_into(part, xg.at[zt], FF)
                else:
                    add_into(part, k.g.at[zt], k.width)
                if d:
                    copy(part, k.zr.at[d - 1], k.at[l] + d, shard=z_peer(d)).start()
            if k is sgu and l == 1:
                for j in (0, 2):
                    pl.semaphore_signal(
                        credit.at[swap_again], inc=1, device_id=swap_to(j), device_id_type=MESH
                    )

    def rs_y_start(k, l):
        @pl.when(core == k.owner)
        def _():
            for d in range(1, SIDE):
                arrived(k.zr.at[d - 1], k.at[l] + d)
            if l == 0:
                for d in range(1, SIDE):
                    sent(k.yr.at[0], k.at[1] + 3 + d)
            own = k.band(l, z)
            if k is sd:
                tot = own[...].astype(f32)
                for d in range(3):
                    tot += k.zr[d].astype(f32)
                k.ys[...] = tot.astype(bf16)
            else:
                step = 256 if k.width % 256 == 0 else 128

                def add(t, c):
                    cols = pl.ds(pl.multiple_of(t * step, 128), step)
                    tot = own[:, cols].astype(f32)
                    for d in range(3):
                        tot += k.zr[d, :, cols].astype(f32)
                    for j in range(SIDE):
                        rows = tot[j * ROWS : j * ROWS + ROWS]
                        rows = jnp.concatenate([rows, jnp.zeros((PAD - ROWS, step), f32)], axis=0)
                        k.ys[j, :, cols] = rows.astype(bf16)
                    return c

                lax.fori_loop(0, k.width // step, add, 0)
            if l == 1:
                for d in range(1, SIDE):
                    pl.semaphore_signal(
                        credit.at[k.again_z], inc=1, device_id={"shard": z_peer(d)}, device_id_type=MESH
                    )
            else:
                pl.semaphore_wait(credit.at[k.again_y], 3)
            for d in (2, 1, 3):
                yt = lax.rem(y + d, SIDE)
                copy(k.ys.at[yt], k.yr.at[d - 1], k.at[l] + 3 + d, shard=y_peer(d)).start()

    def x_targets(l):
        for t in (1, 2, 3):
            other = 1 - sec if t >= 2 else sec
            where = {}
            if t >= 2:
                where["section"] = 1 - sec
            if t % 2:
                where["replica"] = far
            yield t, other == l, where

    def rs_x_start(k, l):
        @pl.when(core == k.owner)
        def _():
            for d in range(1, SIDE):
                arrived(k.yr.at[d - 1], k.at[l] + 3 + d)
            if l == 0:
                xs_sent(k, 1)
            tot = k.ys[y].astype(f32)
            for d in range(3):
                tot += k.yr[d].astype(f32)
            k.xs[...] = tot.astype(bf16)
            if l == 1:
                for d in range(1, SIDE):
                    pl.semaphore_signal(
                        credit.at[k.again_y], inc=1, device_id={"shard": y_peer(d)}, device_id_type=MESH
                    )
            for t, hit, where in x_targets(l):
                @pl.when(hit)
                def _():
                    copy(k.xs, k.xr.at[t - 1], k.at[l] + 6 + t, **where).start()

    def xs_sent(k, l):
        for t, hit, where in x_targets(l):
            @pl.when(hit)
            def _():
                sent(k.xs, k.at[l] + 6 + t)

    def write_out(k, tot):
        if k is sd:
            gd_ref[0] = tot
        elif k is sq:
            gq_ref[0] = tot[0:ROWS, 0:576]
            gk_ref[0] = tot[0:ROWS, 576:768]
            gv_ref[0] = tot[0:ROWS, 768:960]
            gain_ref[...] = tot[0:ROWS, 896:1024]
        else:
            go_ref[0] = tot[0:ROWS, 0:D]

    def rs_end_start(k, l):
        @pl.when((core == k.owner) & (sec == l))
        def _():
            for t in (1, 2, 3):
                arrived(k.xr.at[t - 1], k.at[l] + 6 + t)
            if k is sgu:
                own = k.xs[...].astype(f32) + k.xr[0].astype(f32)
                other = k.xr[1].astype(f32) + k.xr[2].astype(f32)
                own_ref, other_ref = (gg_ref, gu_ref) if l == 0 else (gu_ref, gg_ref)
                k.fs[l] = own.astype(bf16)
                k.fs[1 - l] = other.astype(bf16)
                copy(k.fs, k.fr, k.at[l] + 10, replica=sib).start()
                own_ref[0] = own[0:ROWS]
                other_ref[0] = other[0:ROWS]
            else:
                tot = k.xs[...].astype(f32)
                for t in range(3):
                    tot += k.xr[t].astype(f32)
                k.fs[...] = tot.astype(bf16)
                copy(k.fs, k.fr, k.at[l] + 10, replica=sib).start()
                write_out(k, tot)

    def rs_end(k, l):
        @pl.when((core != k.owner) & (sec == l))
        def _():
            arrived(k.fr, k.at[l] + 10)
            if k is sgu:
                gg_ref[0] = k.fr[0, 0:ROWS].astype(f32)
                gu_ref[0] = k.fr[1, 0:ROWS].astype(f32)
            else:
                write_out(k, k.fr[...].astype(f32))

    def rs_sent():
        for k in (sgu, sd, so, sq):
            @pl.when(core == k.owner)
            def _():
                for l in (1, 0):
                    for d in range(1, SIDE):
                        sent(k.zr.at[0], k.at[l] + d)
                    if k is sgu:
                        for j in range(SIDE):
                            sent(xg.at[j], at_rswap[l] + j)

                    @pl.when(sec == l)
                    def _():
                        sent(k.fs, k.at[l] + 10)

                for d in range(1, SIDE):
                    sent(k.yr.at[0], k.at[0] + 3 + d)
                xs_sent(k, 0)

    at_o = [take(1) for _ in range(2)]
    at_d = [take(1) for _ in range(2)]

    def hand_over(l, value, own_ref, send, recv, at):
        @pl.when(sec == l)
        def _():
            own_ref[0, sec, 0] = value

        @pl.when(sec != l)
        def _():
            send[...] = value
            copy(send, recv, at[l], section=1 - sec).start()

    def hand_over_end(own_ref, send, recv, at):
        for l in range(2):
            @pl.when(sec == l)
            def _():
                arrived(recv, at[l])
                own_ref[0, 1 - sec, 0] = recv[...]

            @pl.when(sec != l)
            def _():
                sent(send, at[l])

    x_start(kq)
    x_start(kgu)
    x_start(ko)
    dx_start()
    xs_[0] = x_ref[sec, 0].astype(f32)
    y_start(kq, 0)
    y_start(kgu, 0)
    dz_start(0)
    y_start(ko, 0)
    z_start(kq, 0)
    z_start(kgu, 0)
    z_start(ko, 0)
    dy_start(0)
    y_start(kq, 1)
    y_start(kgu, 1)
    dz_start(1)
    y_start(ko, 1)
    z_end(kq, 0)
    gather_end(kq, 0)
    project_in(0)
    kv_start(0)
    z_end(kgu, 0)
    z_end(ko, 0)
    d_forward_on(0)
    z_start(kq, 1)
    kv_wait(0)
    attend(0, 0)
    swap_end(0)
    z_start(kgu, 1)
    z_start(ko, 1)
    dy_start(1)
    attend(0, 1)
    z_end(kq, 1)
    attend(0, 2)
    gather_end(ko, 0)
    gather_end(kgu, 0)
    d_gather_end(0)
    out = after_attention(0).astype(bf16)
    xs_[1] = out.astype(f32)
    hand_over(0, out, out_ref, osend, orecv, at_o)
    gather_end(kq, 1)
    project_in(1)
    kv_start(1)
    z_end(kgu, 1)
    z_end(ko, 1)
    d_forward_on(1)
    kv_wait(1)
    attend(1, 0)
    attend(1, 1)
    swap_end(1)
    attend(1, 2)
    gather_end(ko, 1)
    gather_end(kgu, 1)
    d_gather_end(1)
    out = after_attention(1).astype(bf16)
    hand_over(1, out, out_ref, osend, orecv, at_o)
    kv_sent(0)
    kv_sent(1)
    gather_sent()

    dmid = ffn_back(1, dy_ref[sec, 0].astype(f32))
    mid_[1] = dmid
    pair_start(sgu, 1)
    pair_start(sd, 1)
    out_back(1, dmid)
    pair_start(so, 1)
    attention_back(1)
    rs_swap_start(1)
    rs_z_start(sd, 1)
    rs_z_start(so, 1)
    dx = finish_back(1, mid_[1])
    pair_start(sq, 1)
    hand_over(1, dx, dx_ref, dsend, drecv, at_d)
    dkv_sent(1)
    rs_z_start(sgu, 1)
    rs_y_start(sd, 1)
    rs_y_start(so, 1)
    pair_sent(sgu, 1)
    pair_sent(sd, 1)
    dmid = ffn_back(0, dx.astype(bf16).astype(f32))
    mid_[0] = dmid
    pair_start(sgu, 0)
    pair_start(sd, 0)
    rs_z_start(sq, 1)
    rs_y_start(sgu, 1)
    rs_x_start(sd, 1)
    rs_x_start(so, 1)
    pair_sent(so, 1)
    out_back(0, mid_[0])
    pair_start(so, 0)
    attention_back(0)
    rs_swap_start(0)
    rs_z_start(sd, 0)
    rs_z_start(so, 0)
    rs_y_start(sq, 1)
    rs_x_start(sgu, 1)
    pair_sent(sq, 1)
    dx = finish_back(0, mid_[0])
    pair_start(sq, 0)
    hand_over(0, dx, dx_ref, dsend, drecv, at_d)
    rs_x_start(sq, 1)
    rs_end_start(sd, 1)
    rs_end_start(so, 1)
    rs_end_start(sgu, 1)
    rs_z_start(sgu, 0)
    rs_z_start(sq, 0)
    rs_end_start(sq, 1)
    rs_y_start(sd, 0)
    rs_y_start(so, 0)
    rs_y_start(sgu, 0)
    rs_y_start(sq, 0)
    for k in (sd, so, sgu, sq):
        rs_end(k, 1)
    for k in (sd, so, sgu, sq):
        rs_x_start(k, 0)
    for k in (sd, so, sgu, sq):
        rs_end_start(k, 0)
    for k in (sd, so, sgu, sq):
        rs_end(k, 0)
    for k in (sd, so, sgu, sq):
        pair_sent(k, 0)
    dkv_sent(0)
    rs_sent()
    hand_over_end(out_ref, osend, orecv, at_o)
    hand_over_end(dx_ref, dsend, drecv, at_d)
    assert used[0] <= SEMS, used[0]


SEMS = 400


def scratch():
    v = lambda *shape: pltpu.VMEM(shape, bf16)
    w = lambda *shape: pltpu.VMEM(shape, f32)
    widths = (FF, QKV, OUT)
    return [
        *[v(2, SIDE, PAD, n) for n in widths],
        *[v(2, SIDE, BAND, n) for n in (GU, QKV, OUT)], v(2, SIDE, SIDE, FROWS, D),
        v(2, SHARDS * TOK, 384), v(2, SHARDS - 1, TOK, 384),
        w(GROUP, SHARDS * TOK), w(GROUP, 128), w(GROUP, 128),
        w(2, TOK, D), v(2, TOK, D), v(2, HEADS, TOK, 64), v(2, HEADS, TOK, 64),
        w(2, KV_HEADS, GROUP, 1), w(2, TOK, D), v(2, TOK, D), w(2, TOK, GU),
        v(TOK, D), v(HEADS, TOK, 64), w(KV_HEADS, GROUP, 1), w(HEADS, TOK, 64), w(TOK, 384),
        w(TOK, D), v(TOK, D),
        *[v(SIDE, BAND, n) for n in (GU, QKV, OUT)], v(SIDE, SIDE, FROWS, D), v(SIDE, BAND, FF),
        *[v(3, BAND, n) for n in widths], v(3, SIDE, FROWS, D),
        *[v(SIDE, PAD, n) for n in widths], v(SIDE, FROWS, D),
        *[v(3, PAD, n) for n in widths], v(3, FROWS, D),
        *[v(PAD, n) for n in widths], v(FROWS, D),
        *[v(3, PAD, n) for n in widths], v(3, FROWS, D),
        v(2, PAD, FF), v(PAD, QKV), v(PAD, OUT), v(FROWS, D),
        v(2, PAD, FF), v(PAD, QKV), v(PAD, OUT), v(FROWS, D),
        v(TOK, D), v(TOK, D), w(TOK, D), w(TOK, D),
        pltpu.SemaphoreType.DMA((SEMS,)), pltpu.SemaphoreType.DMA((SEMS,)),
        pltpu.SemaphoreType.REGULAR((32,)),
    ]


def kernel(*refs):
    body(*refs)


def local(
    inputs, out_grad, w_query, w_key, w_value, w_out, w_gate, w_up, w_down, gain_attn, gain_ffn
):
    shard_index = lax.axis_index("shard")
    positions = shard_index * TOK + jnp.arange(TOK, dtype=jnp.int32)
    half = HEAD_DIM // 2
    inverse = rope_base ** (-(jnp.arange(half, dtype=f32) * 2.0 / HEAD_DIM))
    angles = positions.astype(f32)[:, None] * inverse[None, :]
    cos, sin = jnp.cos(angles), jnp.sin(angles)
    cos = jnp.concatenate([cos] * 4, axis=1)
    sin = jnp.concatenate([-sin, sin, -sin, sin], axis=1)
    more = ((0, PAD - ROWS), (0, 0))
    p0 = jnp.pad(jnp.concatenate([w_gate[0], w_up[0]], axis=1), more)
    gain_cols = jnp.stack([gain_attn[0], gain_ffn[0]], axis=1)
    pq = jnp.concatenate(
        [w_query[0], w_key[0], w_value[0], gain_cols, jnp.zeros((ROWS, 62), bf16)], axis=1
    )
    pq = jnp.pad(pq, more)
    po = jnp.pad(w_out[0], ((0, PAD - ROWS), (0, OUT - D)))
    whole = pl.BlockSpec(memory_space=pltpu.VMEM)
    shapes = (
        ((1, 2, 1, TOK, D), bf16), ((1, 2, 1, TOK, D), f32),
        ((1, ROWS, 576), f32), ((1, ROWS, 192), f32), ((1, ROWS, 192), f32), ((1, ROWS, 576), f32),
        ((1, ROWS, FF), f32), ((1, ROWS, FF), f32), ((1, FROWS, D), f32), ((ROWS, 128), f32),
    )
    res = pl.pallas_call(
        kernel,
        out_shape=[jax.ShapeDtypeStruct(s, t) for s, t in shapes],
        in_specs=[whole] * 8,
        out_specs=[whole] * len(shapes),
        scratch_shapes=scratch(),
        compiler_params=pltpu.CompilerParams(
            collective_id=0, has_side_effects=True, vmem_limit_bytes=63 * 1024 * 1024
        ),
        name="two_layers",
    )(inputs, out_grad, p0, pq, po, w_down[0], cos, sin)
    out, dx, gq, gk, gv, go, gg, gu, gd, gain = res
    return (out, dx, gq, gk, gv, go, gg, gu, gd, gain[:, 64][None], gain[:, 65][None])


def solution(mesh):
    return jax.shard_map(
        local,
        mesh=mesh,
        in_specs=(
            P(None, "replica", "shard", None),
            P(None, "replica", "shard", None),
            P("section", "shard", None),
            P("section", "shard", None),
            P("section", "shard", None),
            P("section", "shard", None),
            P("section", "shard", None),
            P("section", "shard", None),
            P("section", "shard", None),
            P("section", "shard"),
            P("section", "shard"),
        ),
        out_specs=(
            P("section", None, "replica", "shard", None),
            P("section", None, "replica", "shard", None),
            P("section", "shard", None),
            P("section", "shard", None),
            P("section", "shard", None),
            P("section", "shard", None),
            P("section", "shard", None),
            P("section", "shard", None),
            P("section", "shard", None),
            P("section", "shard"),
            P("section", "shard"),
        ),
        check_vma=False,
    )
```

time: 358 us -> 275 us (0.77)
  Pallas kernels: 341 us -> 257 us
    pallas_call x1, Pallas kernels: 341 us -> 257 us  [local(): pl.pallas_call(kernel, out_shape=[jax.ShapeDtypeStruct(s, t) for s, t in...]
where the time goes in v2:
time: 275 us; the launch traced here: 274 us
  Pallas kernels  257 us (93%)
  local copies, waits for them, and re-layouts  14.9 us (5%)
    pallas_call x1, Pallas kernels, local(): pl.pallas_call(kernel, out_shape=[jax.ShapeDtypeStruct(s, t) for s, t in...  257 us
    unnamed x41, local copies, waits for them, and re-layouts  10.5 us

profile of v2, /device:TPU:1, one launch (start us, length us, event | category | flops | bytes accessed | tf_op | source)
XLA Modules:
  0.0 274.1 jit_solution(2138276136412938639)
XLA Ops:
  0.6 0.0 copy-start.12
  0.7 0.8 copy.46
  1.4 0.8 copy.47
  2.2 0.0 copy-done.12
  2.2 0.8 concatenate.13
  3.1 0.0 copy-start.11
  3.1 0.7 pad.13.refs_3_
  3.7 0.1 copy-done.11
  3.9 0.6 pad.14.refs_4_
  4.5 0.3 fusion.3
  4.8 0.0 copy-start.6
  4.8 0.0 copy-start.7
  4.8 0.8 pad_maximum_fusion
  5.7 0.0 copy-start.1
  5.7 0.1 copy-done.6
  5.7 0.1 copy-done.7
  5.8 0.7 fusion.2.refs_2_
  6.5 0.1 copy-done.1
  6.7 0.0 copy-start.2
  6.7 0.9 copy.49.refs_0_
  7.6 0.1 copy-done.2
  7.6 0.9 copy.50.refs_1_
  8.5 256.6 %two_layers.1 = (bf16[1,2,1,128,576]{4,3,2,1,0:T(8,128)(2,1)}, f32[1,2,1,128,576]{4,3,2,1,0:T(8,128)}, f32[1,36,576]{2,1,0:T(8,128)}, f32[1,36,192]{2,1,0:T(8,12...) custom-call(bf16[2,1,128,576]{3,2,1,0:T(8,128)(2,1)} %copy.49.refs_0, ...), custom_call_target="tpu_custom_call" | custom-call | tf_op jit(solution)/shard_map/two_layers/pallas_call | solution.py:978
  265.1 0.0 copy-start.10
  265.1 0.0 copy-start.14
  265.2 0.0 copy-start.9
  265.2 1.9 copy.51
  267.1 0.0 copy-done.10
  267.1 0.0 copy-start.13
  267.1 0.7 slice_reduce_fusion
  267.8 0.0 copy-done.14
  267.8 0.0 copy-start.8
  267.8 0.7 copy.54
  268.4 0.0 copy-done.13
  268.4 0.7 copy.55
  269.1 0.0 copy-done.9
  269.1 0.7 copy.53
  269.8 0.0 copy-done.8
  269.8 0.7 copy.56
  270.6 0.0 copy-done.4
  270.6 0.9 copy.57
  271.5 0.0 copy-done.3
  271.5 0.9 copy.58
  272.4 0.0 copy-done
  272.4 0.0 copy-start.5
  272.4 1.0 copy.52
  273.4 0.0 copy-done.5
  273.4 0.7 copy.60
  (6 shorter events, 0.0 us)
Async XLA Ops:
  0.6 1.6 copy-start.12
  3.1 0.8 copy-start.11
  4.8 0.9 copy-start.6
  4.8 1.0 copy-start.7
  5.7 1.0 copy-start.1
  6.7 1.0 copy-start.2
  265.1 1.9 copy-start.10
  265.1 2.6 copy-start.14
  265.2 3.9 %copy-start.9 = (f32[1,36,576]{2,1,0:T(8,128)S(1)}, f32[1,36,576]{2,1,0:T(8,128)}, u32[]{:S(2)}) copy-start(f32[1,36,576]{2,1,0:T(8,128)} %get-tuple-element.55) | copy-start | bytes 248836
  267.1 1.4 copy-start.13
  267.8 2.1 copy-start.8
  267.8 2.8 %copy-start.4 = (f32[1,36,1536]{2,1,0:T(8,128)S(1)}, f32[1,36,1536]{2,1,0:T(8,128)}, u32[]{:S(2)}) copy-start(f32[1,36,1536]{2,1,0:T(8,128)} %get-tuple-element.59) | copy-start | bytes 663556
  268.4 3.1 %copy-start.3 = (f32[1,36,1536]{2,1,0:T(8,128)S(1)}, f32[1,36,1536]{2,1,0:T(8,128)}, u32[]{:S(2)}) copy-start(f32[1,36,1536]{2,1,0:T(8,128)} %get-tuple-element.60) | copy-start | bytes 663556
  269.1 3.3 %copy-start = (f32[1,2,1,128,576]{4,3,2,1,0:T(8,128)S(1)}, f32[1,2,1,128,576]{4,3,2,1,0:T(8,128)}, u32[]{:S(2)}) copy-start(f32[1,2,1,128,576]{4,3,2,1,0:T(8,128)} %get-tuple-element.54) | copy-start | bytes 1769476
  272.4 1.1 copy-start.5

commit v3 on v2

--- a/solution.py
+++ b/solution.py
@@ -88,9 +88,9 @@
         used[0] += n
         return at
 
-    def copy(src, dst, at, **dev):
+    def copy(src, dst, at, to=None, **dev):
         return pltpu.make_async_remote_copy(
-            src_ref=src, dst_ref=dst, send_sem=ssem.at[at], recv_sem=rsem.at[at],
+            src_ref=src, dst_ref=dst, send_sem=ssem.at[at], recv_sem=rsem.at[at if to is None else to],
             device_id=dev, device_id_type=MESH,
         )
 
@@ -287,35 +287,90 @@
                 sent(w_d.at[l], at_df[l])
 
     at_kv = [take(SHARDS) for _ in range(2)]
+    at_kvr = [take(4) for _ in range(2)]
     at_dkv = [take(SHARDS) for _ in range(2)]
+    at_dky = [take(4) for _ in range(2)]
     tokens = pl.ds(pl.multiple_of(sh * TOK, TOK), TOK)
+    twice = 2 * SIDE
+
+    def block(l, j):
+        return kv.at[l, pl.ds(pl.multiple_of(j * TOK, TOK), TOK)]
+
+    def relayed(j):
+        gap = lax.div(j, SIDE) - z
+        return ((gap == 2) | (gap == -2)) & (lax.rem(j, SIDE) != y)
 
     def kv_start(l):
         own = kv.at[l, tokens]
 
         def go(d, c):
-            copy(own, own, at_kv[l] + d, shard=sh + d).start()
+            @pl.when(jnp.logical_not(relayed(sh + d)))
+            def _():
+                copy(own, own, at_kv[l] + d, shard=sh + d).start()
+
             return c
 
         lax.fori_loop(1, SHARDS - sh, go, 0)
 
     def kv_wait(l):
+        @pl.when(z >= 2)
+        def _():
+            passing = block(l, sh - twice)
+            arrived(passing, at_kv[l] + twice)
+            for e in range(1, SIDE):
+                yt = lax.rem(y + e, SIDE)
+                copy(passing, passing, at_kvr[l] + e, to=at_kv[l] + twice + yt - y, shard=y_peer(e)).start()
+
         def go(d, c):
-            arrived(kv.at[l, pl.ds(pl.multiple_of((sh - d) * TOK, TOK), TOK)], at_kv[l] + d)
+            @pl.when(d != twice)
+            def _():
+                arrived(block(l, sh - d), at_kv[l] + d)
+
             return c
 
         lax.fori_loop(1, sh + 1, go, 0)
 
     def kv_sent(l):
         def go(d, c):
-            sent(kv.at[l, tokens], at_kv[l] + d)
+            @pl.when(jnp.logical_not(relayed(sh + d)))
+            def _():
+                sent(kv.at[l, tokens], at_kv[l] + d)
+
             return c
 
         lax.fori_loop(1, SHARDS - sh, go, 0)
 
+        @pl.when(z >= 2)
+        def _():
+            for e in range(1, SIDE):
+                sent(kv.at[l, tokens], at_kvr[l] + e)
+
     def dkv_start(l, j):
-        src = kv.at[l, pl.ds(pl.multiple_of(j * TOK, TOK), TOK)]
-        copy(src, dkv_r.at[l, sh - j - 1], at_dkv[l] + sh - j, shard=j).start()
+        away = relayed(j)
+
+        @pl.when(away)
+        def _():
+            e = lax.rem(lax.rem(j, SIDE) - y + SIDE, SIDE)
+            copy(
+                block(l, j), dkv_r.at[l, twice - 1 + e], at_dkv[l] + sh - j,
+                to=at_dky[l] + e, shard=z * SIDE + lax.rem(j, SIDE),
+            ).start()
+
+        @pl.when(jnp.logical_not(away) & (sh - j != twice))
+        def _():
+            copy(block(l, j), dkv_r.at[l, sh - j - 1], at_dkv[l] + sh - j, shard=j).start()
+
+    def dkv_relay(l):
+        @pl.when(z >= 2)
+        def _():
+            passing = block(l, sh - twice)
+            for e in range(1, SIDE):
+                arrived(dkv_r.at[l, twice - 1 + e], at_dky[l] + e)
+            tot = passing[...].astype(f32)
+            for e in range(1, SIDE):
+                tot += dkv_r[l, twice - 1 + e].astype(f32)
+            passing[...] = tot.astype(bf16)
+            copy(passing, dkv_r.at[l, twice - 1], at_dkv[l] + twice, shard=sh - twice).start()
 
     def dkv_sent(l):
         def go(d, c):
@@ -513,8 +568,11 @@
         dkv_acc[...] = kv[l, tokens, :].astype(f32)
 
         def add(d, c):
-            arrived(dkv_r.at[l, d - 1], at_dkv[l] + d)
-            dkv_acc[...] += dkv_r[l, d - 1].astype(f32)
+            @pl.when(jnp.logical_not(relayed(sh + d)))
+            def _():
+                arrived(dkv_r.at[l, d - 1], at_dkv[l] + d)
+                dkv_acc[...] += dkv_r[l, d - 1].astype(f32)
+
             return c
 
         lax.fori_loop(1, SHARDS - sh, add, 0)
@@ -855,6 +913,7 @@
     out_back(1, dmid)
     pair_start(so, 1)
     attention_back(1)
+    dkv_relay(1)
     rs_swap_start(1)
     rs_z_start(sd, 1)
     rs_z_start(so, 1)
@@ -879,6 +938,7 @@
     out_back(0, mid_[0])
     pair_start(so, 0)
     attention_back(0)
+    dkv_relay(0)
     rs_swap_start(0)
     rs_z_start(sd, 0)
     rs_z_start(so, 0)

time: 275 us -> 248 us (0.902)
  Pallas kernels: 257 us -> 230 us
    pallas_call x1, Pallas kernels: 257 us -> 230 us  [local(): pl.pallas_call(kernel, out_shape=[jax.ShapeDtypeStruct(s, t) for s, t in...]
where the time goes in v3:
time: 248 us; the launch traced here: 247 us
  Pallas kernels  230 us (93%)
  local copies, waits for them, and re-layouts  14.9 us (6%)
    pallas_call x1, Pallas kernels, local(): pl.pallas_call(kernel, out_shape=[jax.ShapeDtypeStruct(s, t) for s, t in...  230 us
    unnamed x41, local copies, waits for them, and re-layouts  10.5 us

profile of v3, /device:TPU:1, one launch (start us, length us, event | category | flops | bytes accessed | tf_op | source)
XLA Modules:
  0.0 247.5 jit_solution(12947530383527766036)
XLA Ops:
  0.6 0.0 copy-start.12
  0.7 0.8 copy.46
  1.4 0.8 copy.47
  2.2 0.0 copy-done.12
  2.2 0.8 concatenate.13
  3.1 0.0 copy-start.11
  3.1 0.7 pad.13.refs_3_
  3.7 0.1 copy-done.11
  3.9 0.6 pad.14.refs_4_
  4.5 0.3 fusion.3
  4.8 0.0 copy-start.6
  4.8 0.0 copy-start.7
  4.8 0.8 pad_maximum_fusion
  5.7 0.0 copy-start.1
  5.7 0.1 copy-done.6
  5.7 0.1 copy-done.7
  5.8 0.7 fusion.2.refs_2_
  6.5 0.1 copy-done.1
  6.7 0.0 copy-start.2
  6.7 0.9 copy.49.refs_0_
  7.6 0.1 copy-done.2
  7.6 0.9 copy.50.refs_1_
  8.5 230.0 %two_layers.1 = (bf16[1,2,1,128,576]{4,3,2,1,0:T(8,128)(2,1)}, f32[1,2,1,128,576]{4,3,2,1,0:T(8,128)}, f32[1,36,576]{2,1,0:T(8,128)}, f32[1,36,192]{2,1,0:T(8,12...) custom-call(bf16[2,1,128,576]{3,2,1,0:T(8,128)(2,1)} %copy.49.refs_0, ...), custom_call_target="tpu_custom_call" | custom-call | tf_op jit(solution)/shard_map/two_layers/pallas_call | solution.py:1038
  238.5 0.0 copy-start.10
  238.5 0.0 copy-start.14
  238.5 0.0 copy-start.9
  238.5 1.9 copy.51
  240.4 0.0 copy-done.10
  240.4 0.0 copy-start.13
  240.4 0.7 slice_reduce_fusion
  241.1 0.0 copy-done.14
  241.1 0.0 copy-start.8
  241.1 0.0 copy-start.4
  241.1 0.7 copy.54
  241.8 0.0 copy-done.13
  241.8 0.7 copy.55
  242.4 0.0 copy-done.9
  242.4 0.7 copy.53
  243.2 0.0 copy-done.8
  243.2 0.7 copy.56
  243.9 0.0 copy-done.4
  243.9 0.9 copy.57
  244.8 0.0 copy-done.3
  244.8 0.9 copy.58
  245.7 0.0 copy-done
  245.7 1.0 copy.52
  246.8 0.0 copy-done.5
  246.8 0.7 copy.60
  (6 shorter events, 0.0 us)
Async XLA Ops:
  0.6 1.6 copy-start.12
  3.1 0.8 copy-start.11
  4.8 0.9 copy-start.6
  4.8 1.0 copy-start.7
  5.7 1.0 copy-start.1
  6.7 1.0 copy-start.2
  238.5 1.9 copy-start.10
  238.5 2.6 %copy-start.14 = (f32[1,36,192]{2,1,0:T(8,128)S(1)}, f32[1,36,192]{2,1,0:T(8,128)}, u32[]{:S(2)}) copy-start(f32[1,36,192]{2,1,0:T(8,128)} %get-tuple-element.56) | copy-start | bytes 82948
  238.5 3.9 %copy-start.9 = (f32[1,36,576]{2,1,0:T(8,128)S(1)}, f32[1,36,576]{2,1,0:T(8,128)}, u32[]{:S(2)}) copy-start(f32[1,36,576]{2,1,0:T(8,128)} %get-tuple-element.55) | copy-start | bytes 248836
  240.4 1.4 copy-start.13
  241.1 2.1 copy-start.8
  241.1 2.8 %copy-start.4 = (f32[1,36,1536]{2,1,0:T(8,128)S(1)}, f32[1,36,1536]{2,1,0:T(8,128)}, u32[]{:S(2)}) copy-start(f32[1,36,1536]{2,1,0:T(8,128)} %get-tuple-element.59) | copy-start | bytes 663556
  241.8 3.1 %copy-start.3 = (f32[1,36,1536]{2,1,0:T(8,128)S(1)}, f32[1,36,1536]{2,1,0:T(8,128)}, u32[]{:S(2)}) copy-start(f32[1,36,1536]{2,1,0:T(8,128)} %get-tuple-element.60) | copy-start | bytes 663556
  242.4 3.3 %copy-start = (f32[1,2,1,128,576]{4,3,2,1,0:T(8,128)S(1)}, f32[1,2,1,128,576]{4,3,2,1,0:T(8,128)}, u32[]{:S(2)}) copy-start(f32[1,2,1,128,576]{4,3,2,1,0:T(8,128)} %get-tuple-element.54) | copy-start | bytes 1769476
  245.7 1.1 copy-start.5

commit v4 on v3

--- a/solution.py
+++ b/solution.py
@@ -525,7 +525,7 @@
             dq_[h] = jnp.zeros((TOK, 64), f32)
             dob_[h] = do_h
 
-    def attention_back(l):
+    def attention_back(l, part):
         for g in range(KV_HEADS):
             do = dob_[3 * g : 3 * g + 3].reshape(GROUP, 64).astype(f32)
             og = o_[l, 3 * g : 3 * g + 3].reshape(GROUP, 64).astype(f32)
@@ -555,14 +555,15 @@
                 dkv_start(l, c * SIDE + i)
             return carry
 
-        lax.fori_loop(0, nfull, full, 0)
-        chunk(nfull, True)
-
         def rest(j, carry):
             dkv_start(l, j)
             return carry
 
-        lax.fori_loop(nfull * SIDE, sh, rest, 0)
+        if part == 0:
+            lax.fori_loop(0, nfull, full, 0)
+        else:
+            chunk(nfull, True)
+            lax.fori_loop(nfull * SIDE, sh, rest, 0)
 
     def finish_back(l, dmid_at):
         dkv_acc[...] = kv[l, tokens, :].astype(f32)
@@ -605,8 +606,12 @@
             self.free = credits(2)
             self.again_z, self.again_y = credits(1), credits(1)
 
+            first_y = name == "d"
+            self.i1, self.peer1 = (y, y_peer) if first_y else (z, z_peer)
+            self.i2, self.peer2 = (z, z_peer) if first_y else (y, y_peer)
+
         def band(self, l, j):
-            return self.w.at[l, j] if self.name == "d" else self.w.at[l, j, :, self.cols]
+            return self.w.at[l, :, j] if self.name == "d" else self.w.at[l, j, :, self.cols]
 
     granted = [0]
 
@@ -666,17 +671,17 @@
             if l == 0:
                 pl.semaphore_wait(credit.at[k.again_z], 3)
             for d in (2, 1, 3, 0):
-                zt = lax.rem(z + d, SIDE)
+                zt = lax.rem(k.i1 + d, SIDE)
                 part = k.band(l, zt)
                 if k is sd:
-                    part[...] = (part[...].astype(f32) + k.g[zt].astype(f32)).astype(bf16)
+                    part[...] = (part[...].astype(f32) + k.g[:, zt].astype(f32)).astype(bf16)
                 elif k is sgu:
                     arrived(xg.at[zt], at_rswap[l] + zt)
                     add_into(part, xg.at[zt], FF)
                 else:
                     add_into(part, k.g.at[zt], k.width)
                 if d:
-                    copy(part, k.zr.at[d - 1], k.at[l] + d, shard=z_peer(d)).start()
+                    copy(part, k.zr.at[d - 1], k.at[l] + d, shard=k.peer1(d)).start()
             if k is sgu and l == 1:
                 for j in (0, 2):
                     pl.semaphore_signal(
@@ -691,7 +696,7 @@
             if l == 0:
                 for d in range(1, SIDE):
                     sent(k.yr.at[0], k.at[1] + 3 + d)
-            own = k.band(l, z)
+            own = k.band(l, k.i1)
             if k is sd:
                 tot = own[...].astype(f32)
                 for d in range(3):
@@ -715,13 +720,13 @@
             if l == 1:
                 for d in range(1, SIDE):
                     pl.semaphore_signal(
-                        credit.at[k.again_z], inc=1, device_id={"shard": z_peer(d)}, device_id_type=MESH
+                        credit.at[k.again_z], inc=1, device_id={"shard": k.peer1(d)}, device_id_type=MESH
                     )
             else:
                 pl.semaphore_wait(credit.at[k.again_y], 3)
             for d in (2, 1, 3):
-                yt = lax.rem(y + d, SIDE)
-                copy(k.ys.at[yt], k.yr.at[d - 1], k.at[l] + 3 + d, shard=y_peer(d)).start()
+                yt = lax.rem(k.i2 + d, SIDE)
+                copy(k.ys.at[yt], k.yr.at[d - 1], k.at[l] + 3 + d, shard=k.peer2(d)).start()
 
     def x_targets(l):
         for t in (1, 2, 3):
@@ -740,14 +745,14 @@
                 arrived(k.yr.at[d - 1], k.at[l] + 3 + d)
             if l == 0:
                 xs_sent(k, 1)
-            tot = k.ys[y].astype(f32)
+            tot = k.ys[k.i2].astype(f32)
             for d in range(3):
                 tot += k.yr[d].astype(f32)
             k.xs[...] = tot.astype(bf16)
             if l == 1:
                 for d in range(1, SIDE):
                     pl.semaphore_signal(
-                        credit.at[k.again_y], inc=1, device_id={"shard": y_peer(d)}, device_id_type=MESH
+                        credit.at[k.again_y], inc=1, device_id={"shard": k.peer2(d)}, device_id_type=MESH
                     )
             for t, hit, where in x_targets(l):
                 @pl.when(hit)
@@ -783,15 +788,15 @@
                 k.fs[l] = own.astype(bf16)
                 k.fs[1 - l] = other.astype(bf16)
                 copy(k.fs, k.fr, k.at[l] + 10, replica=sib).start()
-                own_ref[0] = own[0:ROWS]
-                other_ref[0] = other[0:ROWS]
+                own_ref[0] = k.fs[l, 0:ROWS].astype(f32)
+                other_ref[0] = k.fs[1 - l, 0:ROWS].astype(f32)
             else:
                 tot = k.xs[...].astype(f32)
                 for t in range(3):
                     tot += k.xr[t].astype(f32)
                 k.fs[...] = tot.astype(bf16)
                 copy(k.fs, k.fr, k.at[l] + 10, replica=sib).start()
-                write_out(k, tot)
+                write_out(k, k.fs[...].astype(f32))
 
     def rs_end(k, l):
         @pl.when((core != k.owner) & (sec == l))
@@ -912,18 +917,18 @@
     pair_start(sd, 1)
     out_back(1, dmid)
     pair_start(so, 1)
-    attention_back(1)
+    attention_back(1, 0)
+    rs_swap_start(1)
+    attention_back(1, 1)
+    rs_z_start(sd, 1)
     dkv_relay(1)
-    rs_swap_start(1)
-    rs_z_start(sd, 1)
     rs_z_start(so, 1)
+    rs_z_start(sgu, 1)
     dx = finish_back(1, mid_[1])
     pair_start(sq, 1)
     hand_over(1, dx, dx_ref, dsend, drecv, at_d)
     dkv_sent(1)
-    rs_z_start(sgu, 1)
     rs_y_start(sd, 1)
-    rs_y_start(so, 1)
     pair_sent(sgu, 1)
     pair_sent(sd, 1)
     dmid = ffn_back(0, dx.astype(bf16).astype(f32))
@@ -931,38 +936,40 @@
     pair_start(sgu, 0)
     pair_start(sd, 0)
     rs_z_start(sq, 1)
-    rs_y_start(sgu, 1)
-    rs_x_start(sd, 1)
-    rs_x_start(so, 1)
+    rs_y_start(so, 1)
     pair_sent(so, 1)
     out_back(0, mid_[0])
     pair_start(so, 0)
-    attention_back(0)
+    rs_y_start(sgu, 1)
+    attention_back(0, 0)
+    rs_swap_start(0)
+    attention_back(0, 1)
+    rs_x_start(sd, 1)
+    rs_z_start(sd, 0)
     dkv_relay(0)
-    rs_swap_start(0)
-    rs_z_start(sd, 0)
     rs_z_start(so, 0)
+    rs_z_start(sgu, 0)
     rs_y_start(sq, 1)
+    rs_x_start(so, 1)
     rs_x_start(sgu, 1)
     pair_sent(sq, 1)
     dx = finish_back(0, mid_[0])
     pair_start(sq, 0)
     hand_over(0, dx, dx_ref, dsend, drecv, at_d)
+    rs_y_start(sd, 0)
+    rs_z_start(sq, 0)
+    rs_y_start(so, 0)
     rs_x_start(sq, 1)
-    rs_end_start(sd, 1)
-    rs_end_start(so, 1)
-    rs_end_start(sgu, 1)
-    rs_z_start(sgu, 0)
-    rs_z_start(sq, 0)
-    rs_end_start(sq, 1)
-    rs_y_start(sd, 0)
-    rs_y_start(so, 0)
     rs_y_start(sgu, 0)
+    for k in (sd, so, sgu, sq):
+        rs_end_start(k, 1)
+    rs_x_start(sd, 0)
+    rs_x_start(so, 0)
     rs_y_start(sq, 0)
+    rs_x_start(sgu, 0)
     for k in (sd, so, sgu, sq):
         rs_end(k, 1)
-    for k in (sd, so, sgu, sq):
-        rs_x_start(k, 0)
+    rs_x_start(sq, 0)
     for k in (sd, so, sgu, sq):
         rs_end_start(k, 0)
     for k in (sd, so, sgu, sq):

time: 248 us -> 228 us (0.919)
  Pallas kernels: 230 us -> 209 us
    pallas_call x1, Pallas kernels: 230 us -> 209 us  [local(): pl.pallas_call(kernel, out_shape=[jax.ShapeDtypeStruct(s, t) for s, t in...]
where the time goes in v4:
time: 228 us; the launch traced here: 226 us
  Pallas kernels  209 us (92%)
  local copies, waits for them, and re-layouts  14.9 us (7%)
    pallas_call x1, Pallas kernels, local(): pl.pallas_call(kernel, out_shape=[jax.ShapeDtypeStruct(s, t) for s, t in...  209 us
    unnamed x41, local copies, waits for them, and re-layouts  10.5 us

profile of v4, /device:TPU:1, one launch (start us, length us, event | category | flops | bytes accessed | tf_op | source)
XLA Modules:
  0.0 226.2 jit_solution(6217187605077515167)
XLA Ops:
  0.6 0.0 copy-start.12
  0.7 0.8 copy.46
  1.4 0.8 copy.47
  2.2 0.0 copy-done.12
  2.2 0.8 concatenate.13
  3.1 0.0 copy-start.11
  3.1 0.7 pad.13.refs_3_
  3.7 0.1 copy-done.11
  3.9 0.6 pad.14.refs_4_
  4.5 0.3 fusion.3
  4.8 0.0 copy-start.6
  4.8 0.0 copy-start.7
  4.8 0.8 pad_maximum_fusion
  5.7 0.0 copy-start.1
  5.7 0.1 copy-done.6
  5.7 0.1 copy-done.7
  5.8 0.7 fusion.2.refs_2_
  6.5 0.1 copy-done.1
  6.7 0.0 copy-start.2
  6.7 0.9 copy.49.refs_0_
  7.6 0.1 copy-done.2
  7.6 0.9 copy.50.refs_1_
  8.5 208.6 %two_layers.1 = (bf16[1,2,1,128,576]{4,3,2,1,0:T(8,128)(2,1)}, f32[1,2,1,128,576]{4,3,2,1,0:T(8,128)}, f32[1,36,576]{2,1,0:T(8,128)}, f32[1,36,192]{2,1,0:T(8,12...) custom-call(bf16[2,1,128,576]{3,2,1,0:T(8,128)(2,1)} %copy.49.refs_0, ...), custom_call_target="tpu_custom_call" | custom-call | tf_op jit(solution)/shard_map/two_layers/pallas_call | solution.py:1045
  217.2 0.0 copy-start.10
  217.2 0.0 copy-start.14
  217.2 0.0 copy-start.9
  217.2 1.9 copy.51
  219.1 0.0 copy-done.10
  219.1 0.0 copy-start.13
  219.1 0.7 slice_reduce_fusion
  219.8 0.0 copy-done.14
  219.8 0.0 copy-start.8
  219.8 0.0 copy-start.4
  219.8 0.7 copy.54
  220.4 0.0 copy-done.13
  220.5 0.7 copy.55
  221.1 0.0 copy-done.9
  221.1 0.7 copy.53
  221.8 0.0 copy-done.8
  221.8 0.7 copy.56
  222.6 0.0 copy-done.4
  222.6 0.9 copy.57
  223.5 0.0 copy-done.3
  223.5 0.9 copy.58
  224.4 0.0 copy-done
  224.4 1.0 copy.52
  225.5 0.0 copy-done.5
  225.5 0.7 copy.60
  (6 shorter events, 0.0 us)
Async XLA Ops:
  0.6 1.6 copy-start.12
  3.1 0.8 copy-start.11
  4.8 0.9 copy-start.6
  4.8 1.0 copy-start.7
  5.7 1.0 copy-start.1
  6.7 1.0 copy-start.2
  217.2 1.9 copy-start.10
  217.2 2.6 %copy-start.14 = (f32[1,36,192]{2,1,0:T(8,128)S(1)}, f32[1,36,192]{2,1,0:T(8,128)}, u32[]{:S(2)}) copy-start(f32[1,36,192]{2,1,0:T(8,128)} %get-tuple-element.56) | copy-start | bytes 82948
  217.2 3.9 %copy-start.9 = (f32[1,36,576]{2,1,0:T(8,128)S(1)}, f32[1,36,576]{2,1,0:T(8,128)}, u32[]{:S(2)}) copy-start(f32[1,36,576]{2,1,0:T(8,128)} %get-tuple-element.55) | copy-start | bytes 248836
  219.1 1.4 copy-start.13
  219.8 2.1 copy-start.8
  219.8 2.8 %copy-start.4 = (f32[1,36,1536]{2,1,0:T(8,128)S(1)}, f32[1,36,1536]{2,1,0:T(8,128)}, u32[]{:S(2)}) copy-start(f32[1,36,1536]{2,1,0:T(8,128)} %get-tuple-element.59) | copy-start | bytes 663556
  220.5 3.1 %copy-start.3 = (f32[1,36,1536]{2,1,0:T(8,128)S(1)}, f32[1,36,1536]{2,1,0:T(8,128)}, u32[]{:S(2)}) copy-start(f32[1,36,1536]{2,1,0:T(8,128)} %get-tuple-element.60) | copy-start | bytes 663556
  221.1 3.3 %copy-start = (f32[1,2,1,128,576]{4,3,2,1,0:T(8,128)S(1)}, f32[1,2,1,128,576]{4,3,2,1,0:T(8,128)}, u32[]{:S(2)}) copy-start(f32[1,2,1,128,576]{4,3,2,1,0:T(8,128)} %get-tuple-element.54) | copy-start | bytes 1769476
  224.4 1.1 copy-start.5

commit v5 on v4

--- a/solution.py
+++ b/solution.py
@@ -2,6 +2,7 @@
 
 import jax
 import jax.numpy as jnp
+import numpy as np
 from jax import lax
 from jax.experimental import pallas as pl
 from jax.experimental.pallas import tpu as pltpu
@@ -63,15 +64,15 @@
 
 
 def body(
-    x_ref, dy_ref, p0_ref, pq_ref, po_ref, pd_ref, cos_ref, sin_ref,
-    out_ref, dx_ref, gq_ref, gk_ref, gv_ref, go_ref, gg_ref, gu_ref, gd_ref, gain_ref,
+    x_ref, dy_ref, wq_ref, wk_ref, wv_ref, wo_ref, wg_ref, wu_ref, wd_ref, ga_ref, gf_ref, near_ref, far_ref,
+    out_ref, dx_ref, fin_gu, fin_q, fin_o, fin_d,
     stage_gu, stage_q, stage_o, w_gu, w_q, w_o, w_d, kv, dkv_r, scr, mx, acc,
     xs_, a_, q8_, o_, lse_, mid_, bn_, gu_,
     dyb_, dob_, delta_, dq_, dkv_acc, acc2, gain_term,
     g_gu, g_q, g_o, g_d, xg,
     zr_gu, zr_q, zr_o, zr_d, ys_gu, ys_q, ys_o, ys_d, yr_gu, yr_q, yr_o, yr_d,
     xs_gu, xs_q, xs_o, xs_d, xr_gu, xr_q, xr_o, xr_d, fs_gu, fs_q, fs_o, fs_d, fr_gu, fr_q, fr_o, fr_d,
-    osend, orecv, dsend, drecv,
+    osend, orecv, dsend, drecv, pack_gu, cos_ref, sin_ref,
     ssem, rsem, credit,
 ):
     sec = lax.axis_index("section")
@@ -115,6 +116,43 @@
     last = pl.ds(pl.multiple_of(lax.div(sh, SIDE) * CHUNK, CHUNK), CHUNK)
     for l in range(2):
         kv[l, last, :] = jnp.zeros((CHUNK, 384), bf16)
+    def padded(ref, value):
+        ref[0:32] = value[0:32]
+        ref[32:PAD] = jnp.concatenate(
+            [value[32:ROWS].astype(f32), jnp.zeros((PAD - ROWS, value.shape[1]), f32)], axis=0
+        ).astype(bf16)
+
+    @pl.when(core == 1)
+    def _():
+        row16 = lax.broadcasted_iota(jnp.int32, (16, ROWS), 0)
+        gain16 = jnp.where(
+            row16 == 0, ga_ref[...].astype(f32), jnp.where(row16 == 1, gf_ref[...].astype(f32), 0.0)
+        ).astype(bf16)
+        place = lax.broadcasted_iota(jnp.int32, (16, 64), 0) == lax.broadcasted_iota(jnp.int32, (16, 64), 1)
+        gain_cols = dot_tn(gain16, jnp.where(place, 1.0, 0.0).astype(bf16))
+        whole = jnp.concatenate(
+            [wq_ref[0].astype(f32), wk_ref[0].astype(f32), wv_ref[0].astype(f32), gain_cols], axis=1
+        ).astype(bf16)
+        padded(stage_q.at[sec, y], whole)
+        whole = jnp.concatenate([wo_ref[0].astype(f32), jnp.zeros((ROWS, OUT - D), f32)], axis=1).astype(bf16)
+        padded(stage_o.at[sec, y], whole)
+        w_d[sec, z, y] = wd_ref[0]
+
+    for c in range(2):
+        @pl.when((core == 0) & (sec == c))
+        def _():
+            padded(stage_gu.at[sec, y], (wg_ref, wu_ref)[c][0])
+            padded(pack_gu, (wg_ref, wu_ref)[1 - c][0])
+
+    cos1, sin1 = near_ref[:, 0:128], near_ref[:, 128:256]
+    first = far_ref[sh]
+    cos2, sin2 = first[0:1, 0:128], first[0:1, 128:256]
+    low = lax.rem(lax.broadcasted_iota(jnp.int32, (TOK, 128), 1), HEAD_DIM) < HEAD_DIM // 2
+    cos_ref[...] = cos1 * cos2 - sin1 * sin2
+    sine = sin1 * cos2 + cos1 * sin2
+    sin_ref[...] = jnp.where(low, -sine, sine)
+    xs_[0] = x_ref[sec, 0].astype(f32).T
+
     barrier = pltpu.get_barrier_semaphore()
 
     def greet(d, c):
@@ -132,8 +170,8 @@
     theirs = pl.ds(pl.multiple_of((1 - sec) * FF, 128), FF)
 
     class Gather:
-        def __init__(self, owner, send, keep, stage, w, cols, width):
-            self.owner, self.send, self.keep, self.stage, self.w, self.width = owner, send, keep, stage, w, width
+        def __init__(self, owner, send, stage, w, cols, width):
+            self.owner, self.send, self.stage, self.w, self.width = owner, send, stage, w, width
             self.cols = cols
             self.at_x = take(1)
             self.at_y = [take(3) for _ in range(2)]
@@ -143,9 +181,9 @@
         def band(self, l, j):
             return self.w.at[l, j, :, self.cols]
 
-    kgu = Gather(0, p0_ref.at[:, theirs], p0_ref.at[:, mine], stage_gu, w_gu, mine, FF)
-    kq = Gather(1, pq_ref, pq_ref, stage_q, w_q, pl.ds(0, QKV), QKV)
-    ko = Gather(1, po_ref, po_ref, stage_o, w_o, pl.ds(0, OUT), OUT)
+    kgu = Gather(0, pack_gu, stage_gu, w_gu, mine, FF)
+    kq = Gather(1, stage_q.at[sec, y], stage_q, w_q, pl.ds(0, QKV), QKV)
+    ko = Gather(1, stage_o.at[sec, y], stage_o, w_o, pl.ds(0, OUT), OUT)
     at_xd = take(1)
     at_dz = [take(3) for _ in range(2)]
     at_dy = [take(3) for _ in range(2)]
@@ -157,13 +195,11 @@
         @pl.when(core == k.owner)
         def _():
             copy(k.send, k.stage.at[sec, y], k.at_x, section=1 - sec).start()
-            k.stage[sec, y] = k.keep[...]
 
     def dx_start():
         @pl.when(core == 1)
         def _():
-            copy(pd_ref, w_d.at[sec, z, y], at_xd, section=1 - sec).start()
-            w_d[sec, z, y] = pd_ref[...]
+            copy(w_d.at[sec, z, y], w_d.at[sec, z, y], at_xd, section=1 - sec).start()
 
     def y_start(k, l):
         @pl.when(core == k.owner)
@@ -279,7 +315,7 @@
             def _():
                 @pl.when(sec == l)
                 def _():
-                    sent(pd_ref, at_xd)
+                    sent(w_d.at[0, z, y], at_xd)
 
                 for d in range(1, SIDE):
                     sent(w_d.at[l, z, y], at_dz[l] + d - 1)
@@ -765,16 +801,7 @@
             def _():
                 sent(k.xs, k.at[l] + 6 + t)
 
-    def write_out(k, tot):
-        if k is sd:
-            gd_ref[0] = tot
-        elif k is sq:
-            gq_ref[0] = tot[0:ROWS, 0:576]
-            gk_ref[0] = tot[0:ROWS, 576:768]
-            gv_ref[0] = tot[0:ROWS, 768:960]
-            gain_ref[...] = tot[0:ROWS, 896:1024]
-        else:
-            go_ref[0] = tot[0:ROWS, 0:D]
+    fins = {"gu": fin_gu, "q": fin_q, "o": fin_o, "d": fin_d}
 
     def rs_end_start(k, l):
         @pl.when((core == k.owner) & (sec == l))
@@ -784,29 +811,25 @@
             if k is sgu:
                 own = k.xs[...].astype(f32) + k.xr[0].astype(f32)
                 other = k.xr[1].astype(f32) + k.xr[2].astype(f32)
-                own_ref, other_ref = (gg_ref, gu_ref) if l == 0 else (gu_ref, gg_ref)
                 k.fs[l] = own.astype(bf16)
                 k.fs[1 - l] = other.astype(bf16)
                 copy(k.fs, k.fr, k.at[l] + 10, replica=sib).start()
-                own_ref[0] = k.fs[l, 0:ROWS].astype(f32)
-                other_ref[0] = k.fs[1 - l, 0:ROWS].astype(f32)
             else:
                 tot = k.xs[...].astype(f32)
                 for t in range(3):
                     tot += k.xr[t].astype(f32)
                 k.fs[...] = tot.astype(bf16)
                 copy(k.fs, k.fr, k.at[l] + 10, replica=sib).start()
-                write_out(k, k.fs[...].astype(f32))
 
     def rs_end(k, l):
         @pl.when((core != k.owner) & (sec == l))
         def _():
             arrived(k.fr, k.at[l] + 10)
-            if k is sgu:
-                gg_ref[0] = k.fr[0, 0:ROWS].astype(f32)
-                gu_ref[0] = k.fr[1, 0:ROWS].astype(f32)
-            else:
-                write_out(k, k.fr[...].astype(f32))
+            fins[k.name][...] = k.fr[...]
+
+        @pl.when((core == k.owner) & (sec == l))
+        def _():
+            fins[k.name][...] = k.fs[...]
 
     def rs_sent():
         for k in (sgu, sd, so, sq):
@@ -831,6 +854,8 @@
     at_d = [take(1) for _ in range(2)]
 
     def hand_over(l, value, own_ref, send, recv, at):
+        value = value.T.astype(own_ref.dtype)
+
         @pl.when(sec == l)
         def _():
             own_ref[0, sec, 0] = value
@@ -855,7 +880,6 @@
     x_start(kgu)
     x_start(ko)
     dx_start()
-    xs_[0] = x_ref[sec, 0].astype(f32)
     y_start(kq, 0)
     y_start(kgu, 0)
     dz_start(0)
@@ -888,8 +912,8 @@
     gather_end(ko, 0)
     gather_end(kgu, 0)
     d_gather_end(0)
-    out = after_attention(0).astype(bf16)
-    xs_[1] = out.astype(f32)
+    out = after_attention(0)
+    xs_[1] = out.astype(bf16).astype(f32)
     hand_over(0, out, out_ref, osend, orecv, at_o)
     gather_end(kq, 1)
     project_in(1)
@@ -905,13 +929,13 @@
     gather_end(ko, 1)
     gather_end(kgu, 1)
     d_gather_end(1)
-    out = after_attention(1).astype(bf16)
+    out = after_attention(1)
     hand_over(1, out, out_ref, osend, orecv, at_o)
     kv_sent(0)
     kv_sent(1)
     gather_sent()
 
-    dmid = ffn_back(1, dy_ref[sec, 0].astype(f32))
+    dmid = ffn_back(1, dy_ref[sec, 0].astype(f32).T)
     mid_[1] = dmid
     pair_start(sgu, 1)
     pair_start(sd, 1)
@@ -1007,7 +1031,8 @@
         *[v(3, PAD, n) for n in widths], v(3, FROWS, D),
         v(2, PAD, FF), v(PAD, QKV), v(PAD, OUT), v(FROWS, D),
         v(2, PAD, FF), v(PAD, QKV), v(PAD, OUT), v(FROWS, D),
-        v(TOK, D), v(TOK, D), w(TOK, D), w(TOK, D),
+        v(D, TOK), v(D, TOK), w(D, TOK), w(D, TOK),
+        v(PAD, FF), w(TOK, 128), w(TOK, 128),
         pltpu.SemaphoreType.DMA((SEMS,)), pltpu.SemaphoreType.DMA((SEMS,)),
         pltpu.SemaphoreType.REGULAR((32,)),
     ]
@@ -1017,44 +1042,74 @@
     body(*refs)
 
 
+def spread(
+    out_in, dx_in, gu_in, q_in, o_in, d_in,
+    out_ref, dx_ref, gq_ref, gk_ref, gv_ref, go_ref, gg_ref, gu_ref, gd_ref, ga_ref, gf_ref,
+):
+    out_ref[...] = out_in[...]
+    dx_ref[...] = dx_in[...]
+    q = q_in[...].astype(f32)
+    gq_ref[:, 0, :] = q[0:ROWS, 0:576]
+    gk_ref[:, 0, :] = q[0:ROWS, 576:768]
+    gv_ref[:, 0, :] = q[0:ROWS, 768:960]
+    go_ref[:, 0, :] = o_in[...].astype(f32)[0:ROWS, 0:D]
+    gg_ref[:, 0, :] = gu_in[0].astype(f32)[0:ROWS]
+    gu_ref[:, 0, :] = gu_in[1].astype(f32)[0:ROWS]
+    gd_ref[0] = d_in[...].astype(f32)
+    row = lax.broadcasted_iota(jnp.int32, (PAD, 128), 0)
+    lane = lax.broadcasted_iota(jnp.int32, (PAD, 128), 1)
+    rows = dot_tn(q_in[:, 896:1024], jnp.where(row == lane, 1.0, 0.0).astype(bf16))
+    ga_ref[...] = rows[64:65, 0:ROWS]
+    gf_ref[...] = rows[65:66, 0:ROWS]
+
+
+def angle_tables():
+    half = HEAD_DIM // 2
+    inverse = np.float64(rope_base) ** (-(np.arange(half) * 2.0 / HEAD_DIM))
+
+    def table(positions):
+        angles = np.tile(positions[:, None] * inverse[None, :], (1, 4))
+        return jnp.asarray(np.concatenate([np.cos(angles), np.sin(angles)], axis=1).astype(np.float32))
+
+    firsts = np.repeat(np.arange(SHARDS) * TOK, 8)
+    return table(np.arange(TOK)), table(firsts).reshape(SHARDS, 8, 256)
+
+
 def local(
     inputs, out_grad, w_query, w_key, w_value, w_out, w_gate, w_up, w_down, gain_attn, gain_ffn
 ):
-    shard_index = lax.axis_index("shard")
-    positions = shard_index * TOK + jnp.arange(TOK, dtype=jnp.int32)
-    half = HEAD_DIM // 2
-    inverse = rope_base ** (-(jnp.arange(half, dtype=f32) * 2.0 / HEAD_DIM))
-    angles = positions.astype(f32)[:, None] * inverse[None, :]
-    cos, sin = jnp.cos(angles), jnp.sin(angles)
-    cos = jnp.concatenate([cos] * 4, axis=1)
-    sin = jnp.concatenate([-sin, sin, -sin, sin], axis=1)
-    more = ((0, PAD - ROWS), (0, 0))
-    p0 = jnp.pad(jnp.concatenate([w_gate[0], w_up[0]], axis=1), more)
-    gain_cols = jnp.stack([gain_attn[0], gain_ffn[0]], axis=1)
-    pq = jnp.concatenate(
-        [w_query[0], w_key[0], w_value[0], gain_cols, jnp.zeros((ROWS, 62), bf16)], axis=1
-    )
-    pq = jnp.pad(pq, more)
-    po = jnp.pad(w_out[0], ((0, PAD - ROWS), (0, OUT - D)))
+    near, far = angle_tables()
     whole = pl.BlockSpec(memory_space=pltpu.VMEM)
-    shapes = (
-        ((1, 2, 1, TOK, D), bf16), ((1, 2, 1, TOK, D), f32),
-        ((1, ROWS, 576), f32), ((1, ROWS, 192), f32), ((1, ROWS, 192), f32), ((1, ROWS, 576), f32),
-        ((1, ROWS, FF), f32), ((1, ROWS, FF), f32), ((1, FROWS, D), f32), ((ROWS, 128), f32),
-    )
+    turned = ((1, 2, 1, D, TOK), bf16), ((1, 2, 1, D, TOK), f32)
+    shapes = turned + (((2, PAD, FF), bf16), ((PAD, QKV), bf16), ((PAD, OUT), bf16), ((FROWS, D), bf16))
     res = pl.pallas_call(
         kernel,
         out_shape=[jax.ShapeDtypeStruct(s, t) for s, t in shapes],
-        in_specs=[whole] * 8,
+        in_specs=[whole] * 13,
         out_specs=[whole] * len(shapes),
         scratch_shapes=scratch(),
         compiler_params=pltpu.CompilerParams(
             collective_id=0, has_side_effects=True, vmem_limit_bytes=63 * 1024 * 1024
         ),
         name="two_layers",
-    )(inputs, out_grad, p0, pq, po, w_down[0], cos, sin)
-    out, dx, gq, gk, gv, go, gg, gu, gd, gain = res
-    return (out, dx, gq, gk, gv, go, gg, gu, gd, gain[:, 64][None], gain[:, 65][None])
+    )(
+        jnp.swapaxes(inputs, 2, 3), jnp.swapaxes(out_grad, 2, 3), w_query, w_key, w_value, w_out,
+        w_gate, w_up, w_down, gain_attn, gain_ffn, near, far,
+    )
+    rows = lambda n: ((ROWS, 1, n), f32)
+    shapes = turned + (
+        rows(576), rows(192), rows(192), rows(D), rows(FF), rows(FF), ((1, FROWS, D), f32),
+        ((1, ROWS), f32), ((1, ROWS), f32),
+    )
+    out, dx, *grads = pl.pallas_call(
+        spread,
+        out_shape=[jax.ShapeDtypeStruct(s, t) for s, t in shapes],
+        in_specs=[whole] * 6,
+        out_specs=[whole] * 11,
+        name="spread",
+    )(*res)
+    grads[:6] = [jnp.swapaxes(g, 0, 1) for g in grads[:6]]
+    return (jnp.swapaxes(out, 3, 4), jnp.swapaxes(dx, 3, 4), *grads)
 
 
 def solution(mesh):

time: 228 us -> 214 us (0.939)
  local copies, waits for them, and re-layouts: 14.9 us -> 0 us
  Pallas kernels: 209 us -> 212 us
    unnamed x41 -> x0, local copies, waits for them, and re-layouts: 10.5 us -> none
    pallas_call x0 -> x1, Pallas kernels: none -> 2.68 us  [local(): pl.pallas_call(spread, out_shape=[jax.ShapeDtypeStruct(s, t) for s, t in...]
where the time goes in v5:
time: 214 us; the launch traced here: 212 us
  Pallas kernels  212 us (99%)
    pallas_call x1, Pallas kernels, local(): pl.pallas_call(kernel, out_shape=[jax.ShapeDtypeStruct(s, t) for s, t in...  209 us

profile of v5, /device:TPU:1, one launch (start us, length us, event | category | flops | bytes accessed | tf_op | source)
XLA Modules:
  0.0 212.3 jit_solution(5052624956765414844)
XLA Ops:
  0.6 208.9 %two_layers.1 = (bf16[1,2,1,576,128]{4,3,2,1,0:T(8,128)(2,1)}, f32[1,2,1,576,128]{4,3,2,1,0:T(8,128)}, bf16[2,48,1536]{2,1,0:T(8,128)(2,1)}, bf16[48,1024]{1,0:T...) custom-call(bf16[2,1,576,128]{3,2,1,0:T(8,128)(2,1)} %bitcast.10, bf16[2,1,576,128]{3,2,1,0:T(8,128)(2,1)} %bitcast.11, ...), custom_call_target="tpu_custom_call" | custom-call | tf_op jit(solution)/shard_map/two_layers/pallas_call | solution.py:1085
  209.6 2.7 %spread.1 = (bf16[1,2,1,576,128]{4,3,2,1,0:T(8,128)(2,1)}, f32[1,2,1,576,128]{4,3,2,1,0:T(8,128)}, f32[36,1,576]{2,1,0:T(1,128)}, f32[36,1,192]{2,1,0:T(1,128)},...) custom-call(bf16[1,2,1,576,128]{4,3,2,1,0:T(8,128)(2,1)} %get-tuple-, ...), custom_call_target="tpu_custom_call" | custom-call | tf_op jit(solution)/shard_map/spread/pallas_call | solution.py:1104

commit v6 on v5

--- a/solution.py
+++ b/solution.py
@@ -21,10 +21,12 @@
 BAND = SIDE * ROWS
 FROWS = 96
 FBAND = SIDE * FROWS
+PART = 2 * FBAND
 GU = 2 * FF
 QKV = 1024
 OUT = 640
 CHUNK = 512
+HALVES = {1: pl.ds(0, 80), 3: pl.ds(80, BAND - 80)}
 GROUP = 3 * TOK
 
 bf16 = jnp.bfloat16
@@ -175,7 +177,7 @@
             self.cols = cols
             self.at_x = take(1)
             self.at_y = [take(3) for _ in range(2)]
-            self.at_z = [take(3) for _ in range(2)]
+            self.at_z = [take(4) for _ in range(2)]
             self.at_f = [take(4) for _ in range(2)]
 
         def band(self, l, j):
@@ -234,9 +236,28 @@
             for at in range(0, k.width, 128):
                 parts = [k.stage[l, j, :, at : at + 128][0:ROWS].astype(f32) for j in range(SIDE)]
                 own[:, at : at + 128] = jnp.concatenate(parts, axis=0).astype(bf16)
-            for d in (2, 1, 3):
+            for d in (1, 3) if ring(k, l) else (2, 1, 3):
                 copy(own, own, k.at_z[l] + d - 1, shard=z_peer(d)).start()
-            copy(own, own, k.at_f[l], replica=sib).start()
+            pass_on(k, l, z, 0)
+
+    def ring(k, l):
+        return not (k is kq and l == 0)
+
+    def pass_on(k, l, j, d):
+        got = k.band(l, j)
+        copy(got, got, k.at_f[l] + d, replica=sib).start()
+        if k is kgu:
+            copy(got, got, at_swap[l] + j, **swap_to(j)).start()
+
+    def z_mid(k, l):
+        @pl.when(core == k.owner)
+        def _():
+            for d in (1, 3):
+                got = k.band(l, z_from(d))
+                arrived(got, k.at_z[l] + d - 1)
+                half = got.at[HALVES[d]]
+                copy(half, half, k.at_z[l] + (1 if d == 1 else 3), shard=z_peer(d)).start()
+                pass_on(k, l, z_from(d), d)
 
     def dy_start(l):
         @pl.when(core == 1)
@@ -250,17 +271,20 @@
     def z_end(k, l):
         @pl.when(core == k.owner)
         def _():
-            for d in (1, 3, 2):
-                got = k.band(l, z_from(d))
-                arrived(got, k.at_z[l] + d - 1)
-                copy(got, got, k.at_f[l] + d, replica=sib).start()
-            if k is kgu:
-                for j in range(SIDE):
-                    got = k.band(l, j)
-                    copy(got, got, at_swap[l] + j, **swap_to(j)).start()
+            if ring(k, l):
+                got = k.band(l, z_from(2))
+                arrived(got.at[HALVES[1]], k.at_z[l] + 1)
+                arrived(got.at[HALVES[3]], k.at_z[l] + 3)
+                pass_on(k, l, z_from(2), 2)
+            else:
+                for d in (1, 3, 2):
+                    arrived(k.band(l, z_from(d)), k.at_z[l] + d - 1)
+                    pass_on(k, l, z_from(d), d)
 
     def swap_to(j):
-        return {"section": 1 - sec} if j < 2 else {"section": 1 - sec, "replica": far}
+        if isinstance(j, int):
+            return {"section": 1 - sec} if j < 2 else {"section": 1 - sec, "replica": far}
+        return {"section": 1 - sec, "replica": jnp.where(j < 2, rep, far)}
 
     def swap_end(l):
         @pl.when(core == 0)
@@ -303,8 +327,12 @@
 
                     for d in range(1, SIDE):
                         sent(k.stage.at[l, y], k.at_y[l] + d - 1)
-                        sent(k.band(l, z), k.at_z[l] + d - 1)
+                        if not ring(k, l) or d != 2:
+                            sent(k.band(l, z), k.at_z[l] + d - 1)
                         sent(k.band(l, z), k.at_f[l] + d)
+                    if ring(k, l):
+                        sent(k.band(l, z).at[HALVES[1]], k.at_z[l] + 1)
+                        sent(k.band(l, z).at[HALVES[3]], k.at_z[l] + 3)
                     sent(k.band(l, z), k.at_f[l])
                     if k is kgu:
                         for j in range(SIDE):
@@ -504,18 +532,18 @@
         acc2[...] = mid
 
         def tile(t, c):
-            gcols = pl.ds(pl.multiple_of(t * FBAND, 128), FBAND)
-            ucols = pl.ds(pl.multiple_of(FF + t * FBAND, 128), FBAND)
+            gcols = pl.ds(pl.multiple_of(t * PART, 128), PART)
+            ucols = pl.ds(pl.multiple_of(FF + t * PART, 128), PART)
             bn = bn_[l]
-            gt = dot(bn, w_gu[l, :, :, gcols].reshape(D, FBAND))
-            up = dot(bn, w_gu[l, :, :, ucols].reshape(D, FBAND))
+            gt = dot(bn, w_gu[l, :, :, gcols].reshape(D, PART))
+            up = dot(bn, w_gu[l, :, :, ucols].reshape(D, PART))
             gu_[l, :, gcols] = gt
             gu_[l, :, ucols] = up
             hid = (gt * jax.nn.sigmoid(gt) * up).astype(bf16)
-            acc2[...] += dot(hid, w_d[l, t].reshape(FBAND, D))
+            acc2[...] += dot(hid, w_d[l, pl.ds(2 * t, 2)].reshape(PART, D))
             return c
 
-        lax.fori_loop(0, SIDE, tile, 0)
+        lax.fori_loop(0, FF // PART, tile, 0)
         return acc2[...]
 
     def ffn_back(l, dy):
@@ -523,25 +551,25 @@
         acc2[...] = jnp.zeros_like(acc2)
 
         def tile(t, c):
-            gcols = pl.ds(pl.multiple_of(t * FBAND, 128), FBAND)
-            ucols = pl.ds(pl.multiple_of(FF + t * FBAND, 128), FBAND)
+            gcols = pl.ds(pl.multiple_of(t * PART, 128), PART)
+            ucols = pl.ds(pl.multiple_of(FF + t * PART, 128), PART)
             dyb = dyb_[...]
             bn = bn_[l]
-            wd = w_d[l, t].reshape(FBAND, D)
+            wd = w_d[l, pl.ds(2 * t, 2)].reshape(PART, D)
             dhid = dot_nt(dyb, wd).astype(bf16).astype(f32)
             gt, up = gu_[l, :, gcols], gu_[l, :, ucols]
             s = jax.nn.sigmoid(gt)
             hid = (gt * s * up).astype(bf16)
-            g_d[t] = dot_tn(hid, dyb).astype(bf16).reshape(SIDE, FROWS, D)
+            g_d[pl.ds(2 * t, 2)] = dot_tn(hid, dyb).astype(bf16).reshape(2, SIDE, FROWS, D)
             dgt = (dhid * up * s * (1.0 + gt * (1.0 - s))).astype(bf16)
             dup = (dhid * gt * s).astype(bf16)
-            g_gu[:, :, gcols] = dot_tn(bn, dgt).astype(bf16).reshape(SIDE, BAND, FBAND)
-            g_gu[:, :, ucols] = dot_tn(bn, dup).astype(bf16).reshape(SIDE, BAND, FBAND)
-            acc2[...] += dot_nt(dgt, w_gu[l, :, :, gcols].reshape(D, FBAND))
-            acc2[...] += dot_nt(dup, w_gu[l, :, :, ucols].reshape(D, FBAND))
+            g_gu[:, :, gcols] = dot_tn(bn, dgt).astype(bf16).reshape(SIDE, BAND, PART)
+            g_gu[:, :, ucols] = dot_tn(bn, dup).astype(bf16).reshape(SIDE, BAND, PART)
+            acc2[...] += dot_nt(dgt, w_gu[l, :, :, gcols].reshape(D, PART))
+            acc2[...] += dot_nt(dup, w_gu[l, :, :, ucols].reshape(D, PART))
             return c
 
-        lax.fori_loop(0, SIDE, tile, 0)
+        lax.fori_loop(0, FF // PART, tile, 0)
         dbn = acc2[...]
         mid = mid_[l]
         r = factor_of(mid)
@@ -565,7 +593,8 @@
         for g in range(KV_HEADS):
             do = dob_[3 * g : 3 * g + 3].reshape(GROUP, 64).astype(f32)
             og = o_[l, 3 * g : 3 * g + 3].reshape(GROUP, 64).astype(f32)
-            delta_[g] = jnp.sum(do * og, axis=1, keepdims=True)
+            if part == 0:
+                delta_[g] = jnp.sum(do * og, axis=1, keepdims=True)
 
         def chunk(c, masked):
             kvb = kv[l, keys_at(c), :]
@@ -896,19 +925,22 @@
     gather_end(kq, 0)
     project_in(0)
     kv_start(0)
-    z_end(kgu, 0)
-    z_end(ko, 0)
+    z_mid(kgu, 0)
+    z_mid(ko, 0)
     d_forward_on(0)
     z_start(kq, 1)
     kv_wait(0)
+    z_end(kgu, 0)
+    z_end(ko, 0)
     attend(0, 0)
-    swap_end(0)
     z_start(kgu, 1)
     z_start(ko, 1)
     dy_start(1)
+    z_mid(kq, 1)
     attend(0, 1)
+    swap_end(0)
+    attend(0, 2)
     z_end(kq, 1)
-    attend(0, 2)
     gather_end(ko, 0)
     gather_end(kgu, 0)
     d_gather_end(0)
@@ -918,10 +950,12 @@
     gather_end(kq, 1)
     project_in(1)
     kv_start(1)
+    z_mid(kgu, 1)
+    z_mid(ko, 1)
+    d_forward_on(1)
+    kv_wait(1)
     z_end(kgu, 1)
     z_end(ko, 1)
-    d_forward_on(1)
-    kv_wait(1)
     attend(1, 0)
     attend(1, 1)
     swap_end(1)

time: 214 us -> 207 us (0.967)
  Pallas kernels: 212 us -> 206 us
    pallas_call x1, Pallas kernels: 209 us -> 203 us  [local(): pl.pallas_call(kernel, out_shape=[jax.ShapeDtypeStruct(s, t) for s, t in...]
where the time goes in v6:
time: 207 us; the launch traced here: 206 us
  Pallas kernels  206 us (100%)
    pallas_call x1, Pallas kernels, local(): pl.pallas_call(kernel, out_shape=[jax.ShapeDtypeStruct(s, t) for s, t in...  203 us

profile of v6, /device:TPU:1, one launch (start us, length us, event | category | flops | bytes accessed | tf_op | source)
XLA Modules:
  0.0 206.2 jit_solution(17912217770969984172)
XLA Ops:
  0.6 202.9 %two_layers.1 = (bf16[1,2,1,576,128]{4,3,2,1,0:T(8,128)(2,1)}, f32[1,2,1,576,128]{4,3,2,1,0:T(8,128)}, bf16[2,48,1536]{2,1,0:T(8,128)(2,1)}, bf16[48,1024]{1,0:T...) custom-call(bf16[2,1,576,128]{3,2,1,0:T(8,128)(2,1)} %bitcast.10, bf16[2,1,576,128]{3,2,1,0:T(8,128)(2,1)} %bitcast.11, ...), custom_call_target="tpu_custom_call" | custom-call | tf_op jit(solution)/shard_map/two_layers/pallas_call | solution.py:1119
  203.6 2.7 %spread.1 = (bf16[1,2,1,576,128]{4,3,2,1,0:T(8,128)(2,1)}, f32[1,2,1,576,128]{4,3,2,1,0:T(8,128)}, f32[36,1,576]{2,1,0:T(1,128)}, f32[36,1,192]{2,1,0:T(1,128)},...) custom-call(bf16[1,2,1,576,128]{4,3,2,1,0:T(8,128)(2,1)} %get-tuple-, ...), custom_call_target="tpu_custom_call" | custom-call | tf_op jit(solution)/shard_map/spread/pallas_call | solution.py:1138

commit v7 on v6

--- a/solution.py
+++ b/solution.py
@@ -999,21 +999,21 @@
     out_back(0, mid_[0])
     pair_start(so, 0)
     rs_y_start(sgu, 1)
+    rs_swap_start(0)
     attention_back(0, 0)
-    rs_swap_start(0)
     attention_back(0, 1)
     rs_x_start(sd, 1)
     rs_z_start(sd, 0)
     dkv_relay(0)
     rs_z_start(so, 0)
     rs_z_start(sgu, 0)
-    rs_y_start(sq, 1)
-    rs_x_start(so, 1)
-    rs_x_start(sgu, 1)
     pair_sent(sq, 1)
     dx = finish_back(0, mid_[0])
     pair_start(sq, 0)
     hand_over(0, dx, dx_ref, dsend, drecv, at_d)
+    rs_y_start(sq, 1)
+    rs_x_start(so, 1)
+    rs_x_start(sgu, 1)
     rs_y_start(sd, 0)
     rs_z_start(sq, 0)
     rs_y_start(so, 0)

time: 207 us -> 205 us (level)
  no operation moved by 1% of the time
where the time goes in v7:
time: 205 us
  Pallas kernels  204 us (100%)
    pallas_call x1, Pallas kernels, local(): pl.pallas_call(kernel, out_shape=[jax.ShapeDtypeStruct(s, t) for s, t in...  202 us

profile of v7, /device:TPU:1, one launch (start us, length us, event | category | flops | bytes accessed | tf_op | source)
XLA Modules:
  0.0 205.1 jit_solution(12013131780737118500)
XLA Ops:
  0.6 201.8 %two_layers.1 = (bf16[1,2,1,576,128]{4,3,2,1,0:T(8,128)(2,1)}, f32[1,2,1,576,128]{4,3,2,1,0:T(8,128)}, bf16[2,48,1536]{2,1,0:T(8,128)(2,1)}, bf16[48,1024]{1,0:T...) custom-call(bf16[2,1,576,128]{3,2,1,0:T(8,128)(2,1)} %bitcast.10, bf16[2,1,576,128]{3,2,1,0:T(8,128)(2,1)} %bitcast.11, ...), custom_call_target="tpu_custom_call" | custom-call | tf_op jit(solution)/shard_map/two_layers/pallas_call | solution.py:1119
  202.4 2.7 %spread.1 = (bf16[1,2,1,576,128]{4,3,2,1,0:T(8,128)(2,1)}, f32[1,2,1,576,128]{4,3,2,1,0:T(8,128)}, f32[36,1,576]{2,1,0:T(1,128)}, f32[36,1,192]{2,1,0:T(1,128)},...) custom-call(bf16[1,2,1,576,128]{4,3,2,1,0:T(8,128)(2,1)} %get-tuple-, ...), custom_call_target="tpu_custom_call" | custom-call | tf_op jit(solution)/shard_map/spread/pallas_call | solution.py:1138
